TPU v7x, 1024 devices: a whole 4x4x32 slice. The times are simulated.
1024 devices in a mesh: comp: 4 (over y), tile: 32 (over z_lo, core), lev: 8 (over z_hi, x).
Axes of the slice: x: 4, y: 4, z: 32 (z_hi: 2, z_lo: 16; z = z_hi * 16 + z_lo), core: 2. Of those that a mesh axis runs over, the one named last changes fastest.
Arguments:
- thermal_anomaly: float32 [4, 80, 16384], P('comp', 'lev', 'tile'), may hold values from -6 to 6
- right_face_transport_ratio: float32 [4, 80, 16384], P('comp', 'lev', 'tile'), may hold values from -0.45 to 0.45
- species_ratios: float32 [4, 40, 80, 16384], P('comp', None, 'lev', 'tile'), may hold values from 0.1 to 3
- lateral_spreading_number: float32 [4, 80, 16384], P('comp', 'lev', 'tile'), may hold values from 0.05 to 0.2
- depth_physics_operator: float32 [4, 80, 80], P('comp'), may hold values from -1 to 1, as said below
- exchange_weight_table: float32 [16384, 4], P('tile'), may hold values from 0.05 to 0.5
- sky_point_of_entry: int32 [16384, 4], P('tile'), may hold values from 0 to 16383, as said below
- water_indicator: int32 [16384], P('tile'), may hold values 0 or 1
Outputs:
- thermal_anomaly_ending: float32 [4, 80, 16384], P('comp', 'lev', 'tile')
- species_ratios_ending: float32 [4, 40, 80, 16384], P('comp', None, 'lev', 'tile')
Inputs may be any that keep to these rules, and one draw needn't show every extreme that they name: The ocean cells of each block of 512 (cells b * 512 to (b + 1) * 512 - 1) take their sources near the matching cells of one atmosphere block p(b), p a permutation of the blocks: sky_point_of_entry[j, k] lies cyclically within 128 cells of p(b) * 512 + (j mod 512). `depth_physics_operator`: each matrix has diagonal entries between 0.5 and 1.
All inputs are finite; a program needn't handle non-finite values. No bound on the sum of `water_indicator` on one device may be relied on, other than what follows from the above.
Results may differ from a plain program's by a relative error of at most 0.0003.
Values sent between devices are 32-bit elements; how exact they have to be, the bound alone decides.
A program may use at most 32 MiB of HBM per device.

v0:
```python
import jax
import jax.numpy as jnp
from jax import lax
from jax.sharding import PartitionSpec as P

NFLUX = 4


def extended(x, sides, width):
    for axis, dim in sides:
        devices, length = (lax.axis_size(axis), x.shape[dim])
        up = [(i, (i + 1) % devices) for i in range(devices)]
        down = [(j, i) for i, j in up]
        last = lax.slice_in_dim(x, length - width, length, axis=dim)
        first = lax.slice_in_dim(x, 0, width, axis=dim)
        before = lax.ppermute(last, axis, up)
        after = lax.ppermute(first, axis, down)
        x = jnp.concatenate([before, x, after], axis=dim)
    return x


def passed_along(value, axis, steps):
    count = lax.axis_size(axis)
    first, last = (max(0, -steps), min(count, count - steps))
    return lax.ppermute(value, axis, [(source, source + steps) for source in range(first, last)])


def advance(padded, lateral_spreading_number):
    middle = padded[..., 1:-1]
    before = padded[..., :-2]
    after = padded[..., 2:]
    speed = middle[:, 1:2]
    speed_left = before[:, 1:2]
    flux_right = jnp.maximum(speed, 0.0) * middle + jnp.minimum(speed, 0.0) * after
    flux_left = jnp.maximum(speed_left, 0.0) * before + jnp.minimum(speed_left, 0.0) * middle
    tendency = -(flux_right - flux_left)
    thermal_energy = middle[:, 0]
    heat_next = thermal_energy + (
        tendency[:, 0]
        + lateral_spreading_number * (before[:, 0] - 2.0 * thermal_energy + after[:, 0])
    )
    tracer_next = middle[:, 2:] + tendency[:, 2:]
    return jnp.concatenate([heat_next[:, None], speed, tracer_next], axis=1)


def body(
    thermal_anomaly,
    right_face_transport_ratio,
    species_ratios,
    lateral_spreading_number,
    depth_physics_operator,
    exchange_weight_table,
    sky_point_of_entry,
    water_indicator,
):
    sections = lax.axis_size("comp")
    is_ocean = lax.axis_index("comp") >= sections // 2
    joined_quantities = jnp.concatenate(
        [thermal_anomaly[:, None], right_face_transport_ratio[:, None], species_ratios], axis=1
    )
    for substep in range(2):
        padded = extended(joined_quantities, (("tile", 3),), 1)
        advanced = advance(padded, lateral_spreading_number)
        if substep == 0:
            joined_quantities = advanced
        else:
            joined_quantities = jnp.where(is_ocean, joined_quantities, advanced)
    column = joined_quantities[0, 0]
    level_count = column.shape[0]
    offset = lax.axis_index("lev") * level_count
    matrix = depth_physics_operator[0]
    my_columns = lax.dynamic_slice_in_dim(matrix, offset, level_count, 1)
    blended_profiles = lax.psum_scatter(
        jnp.dot(
            my_columns, column, precision=lax.Precision.HIGHEST, preferred_element_type=jnp.float32
        ),
        "lev",
        scatter_dimension=0,
        tiled=True,
    )
    surface = jnp.concatenate(
        [blended_profiles[0:1], joined_quantities[0, 2 : 2 + NFLUX - 1, 0]], 0
    )
    whole = lax.all_gather(surface, "tile", axis=1, tiled=True)
    received = passed_along(whole, "comp", sections // 2)
    picked = received[:, sky_point_of_entry]
    remapped = jnp.sum(picked * exchange_weight_table, -1)
    updated = surface + 0.5 * (remapped - surface)
    at_sea = jnp.logical_and(
        jnp.logical_and(is_ocean, lax.axis_index("lev") == 0), water_indicator == 1
    )
    renewed_interface_values = jnp.where(at_sea[None, :], updated, surface)
    thermal_anomaly_ending = blended_profiles.at[0].set(renewed_interface_values[0])[None]
    species_ratios_ending = (
        joined_quantities[:, 2:].at[0, 0 : NFLUX - 1, 0].set(renewed_interface_values[1:])
    )
    return (thermal_anomaly_ending, species_ratios_ending)


def solution(mesh):
    in_specs = (
        P("comp", "lev", "tile"),
        P("comp", "lev", "tile"),
        P("comp", None, "lev", "tile"),
        P("comp", "lev", "tile"),
        P("comp", None, None),
        P("tile", None),
        P("tile", None),
        P("tile"),
    )
    out_specs = (P("comp", "lev", "tile"), P("comp", None, "lev", "tile"))
    return jax.shard_map(body, mesh=mesh, in_specs=in_specs, out_specs=out_specs, check_vma=False)
```

profile of v0, /device:TPU:24, one launch (start us, length us, event | category | flops | bytes accessed | tf_op | source)
XLA Modules:
  0.0 464.5 jit_solution(15823416539695195699)
XLA Ops:
  7.2 0.0 copy-start
  7.2 0.0 all-reduce.3.cloned.1.call-start
  7.2 2.0 copy.245
  9.3 0.0 copy-start.7
  9.3 0.7 fusion.8
  10.0 0.6 fusion.38
  10.6 25.8 %collective-permute-start = (f32[1,42,10,1]{3,0,2,1:T(1,128)S(1)}, f32[1,42,10,1]{3,0,2,1:T(1,128)S(1)}, u32[]{:S(2)}, u32[]{:S(2)}) collective-permute-start(f32[1,42,10,1]{3,0,2,1:T(1,128)S(1)} %get-tuple-element.56), channel_id=1, source_target_pairs={{8,0},{16,8},{24,16},{32,24},{40,32},{48,40},{56,48},{64,56},{72,6... | collective-permute-start | bytes 5048 | tf_op jit(solution)/shard_map/ppermute | solution.py:17
  36.5 1.9 collective-permute-start.1
  38.5 1.4 collective-permute-done
  39.9 21.1 %collective-permute-done.1 = f32[1,42,10,1]{3,0,2,1:T(1,128)S(1)} collective-permute-done((f32[1,42,10,1]{3,0,2,1:T(1,128)S(1)}, f32[1,42,10,1]{3,0,2,1:T(1,128)S(1)}, u32[]{:S(2)}, u32[]{:S(2)}) %collective-permute-start.1) | collective-permute-done | bytes 1712 | tf_op jit(solution)/shard_map/ppermute | solution.py:16
  61.0 6.0 %fusion.5 = (f32[1,42,10,513]{3,0,2,1:T(1,128)S(1)}, f32[1,42,10,513]{3,0,2,1:T(1,128)S(1)}) fusion(f32[1,1,10,512]{3,0,2,1:T(1,128)S(1)} %bitcast.90, f32[1,42,10,1]{3,0,2,1:T(1,128)S(1)} %collective-permute-done, f32[1,40,10,512]{3,0,2,1:T(1,128)S(1)} %copy.245, f32[1,1,10,512]{3,0,2,1:T(1,128)S(1)} %bitcast.100, ...), kind=kLoop, calls=%fused_computation.11 | loop fusion | flops 1292760 | bytes 2587200 | tf_op jit(solution)/shard_map/concatenate | solution.py:18
  67.0 0.0 copy-start.2
  67.0 2.4 fusion.17
  69.5 0.0 copy-start.5
  69.5 1.1 slice_add_fusion.1
  70.7 0.1 fusion.34
  70.8 0.7 fusion.9
  71.5 0.6 fusion.37
  72.1 1.9 collective-permute-start.2
  74.0 2.6 collective-permute-start.3
  76.7 0.1 copy.251
  76.8 0.2 reshape.390
  77.0 0.1 copy.253
  77.2 1.3 dynamic-slice.16
  79.1 18.4 %collective-permute-done.3 = f32[1,42,10,1]{3,0,2,1:T(1,128)S(1)} collective-permute-done((f32[1,42,10,1]{3,0,2,1:T(1,128)S(1)}, f32[1,42,10,1]{3,0,2,1:T(1,128)S(1)}, u32[]{:S(2)}, u32[]{:S(2)}) %collective-permute-start.3) | collective-permute-done | bytes 1712 | tf_op jit(solution)/shard_map/ppermute | solution.py:16
  97.5 6.0 %fusion.7 = (f32[1,42,10,513]{3,0,2,1:T(1,128)S(1)}, f32[1,42,10,513]{3,0,2,1:T(1,128)S(1)}) fusion(f32[1,1,10,512]{3,0,2,1:T(1,128)S(1)} %bitcast.93, f32[1,42,10,1]{3,0,2,1:T(1,128)S(1)} %collective-permute-done.2, f32[1,40,10,512]{3,0,2,1:T(1,128)S(1)} %slice_add_fusion.1, f32[1,1,10,512]{3,0,2,1:T(1,128)S(1)} %bitcast.97, ...), kind=kLoop, calls=%fused_computation.13 | loop fusion | flops 1292760 | bytes 2587200 | tf_op jit(solution)/shard_map/concatenate | solution.py:18
  103.5 2.4 fusion.18
  106.0 0.8 slice_add_fusion
  106.8 0.1 add_bitcast_fusion
  106.9 0.7 fusion.10
  107.7 0.0 copy-start.8
  107.7 0.3 copy_select_fusion
  108.0 1.1 fusion.19
  109.1 0.0 all-reduce.3.cloned.1.call-update
  109.2 226.8 %all-reduce.3.cloned.1.call-done = f32[80,512]{1,0:T(8,128)} async-done(((f32[80,512]{1,0:T(8,128)}), f32[80,512]{1,0:T(8,128)}) %all-reduce.3.cloned.1.call-update) | async-done | bytes 163856
  336.0 0.7 constant_dynamic-slice_fusion
  336.8 89.8 %all_gather.3 = f32[4,16384]{1,0:T(4,128)S(1)} all-gather(f32[4,512]{1,0:T(4,128)S(1)} %pad_maximum_fusion.7), channel_id=1, replica_groups=mesh['comp'=4,'tile'=32,'lev'=8] {'tile'}, dimensions={1}, use_global_device_ids=true | all-gather | bytes 270336 | tf_op jit(solution)/shard_map/all_gather | solution.py:84
  426.6 1.3 collective-permute-start.4
  427.9 0.8 dynamic-slice_bitcast_fusion
  428.7 9.8 %collective-permute-done.4 = f32[4,16384]{1,0:T(4,128)S(1)} collective-permute-done((f32[4,16384]{1,0:T(4,128)S(1)}, f32[4,16384]{1,0:T(4,128)S(1)}, u32[]{:S(2)}, u32[]{:S(2)}) %collective-permute-start.4) | collective-permute-done | bytes 262176 | tf_op jit(solution)/shard_map/ppermute | solution.py:25
  438.6 5.0 %copy.252 = f32[4,16384]{0,1:T(8,128)} copy(f32[4,16384]{1,0:T(4,128)S(1)} %collective-permute-done.4) | data formatting | bytes 524288 | tf_op jit(solution)/shard_map/ppermute | solution.py:25
  443.6 8.9 %gather_fusion = f32[2048,4]{1,0:T(8,128)S(1)} fusion(f32[4,16384]{0,1:T(8,128)} %copy.252, s32[2048]{0:T(1024)S(1)} %broadcast_clamp_fusion), kind=kCustom, calls=%fused_computation | custom fusion | bytes 73728 | tf_op jit(solution)/shard_map/gather | solution.py:86
  452.5 2.8 multiply_reduce_fusion
  455.3 0.1 copy.254
  455.4 0.1 scatter.6
  455.5 0.6 copy.256
  456.1 0.1 scatter.9
  456.2 1.4 copy.257
  (32 shorter events, 0.2 us)
Async XLA Ops:
  7.2 100.8 %copy-start = (f32[1,80,80]{2,1,0:T(8,128)S(1)}, f32[1,80,80]{2,1,0:T(8,128)}, u32[]{:S(2)}) copy-start(f32[1,80,80]{2,1,0:T(8,128)} %param.16) | copy-start | bytes 76804
  7.2 2.1 copy-start.3
  7.2 2.1 copy-start.4
  7.2 328.8 %all-reduce.3.cloned.1.call-start = ((), (), s32[]{:S(2)}) async-start(), calls=%async_computation | async-start | bytes 327680
  9.3 29.2 %copy-start.7 = (s32[512,4]{0,1:T(4,128)S(1)}, s32[512,4]{0,1:T(4,128)}, u32[]{:S(2)}) copy-start(s32[512,4]{0,1:T(4,128)} %param.18) | copy-start | bytes 24580
  10.6 29.3 %collective-permute-start = (f32[1,42,10,1]{3,0,2,1:T(1,128)S(1)}, f32[1,42,10,1]{3,0,2,1:T(1,128)S(1)}, u32[]{:S(2)}, u32[]{:S(2)}) collective-permute-start(f32[1,42,10,1]{3,0,2,1:T(1,128)S(1)} %get-tuple-element.56), channel_id=1, source_target_pairs={{8,0},{16,8},{24,16},{32,24},{40,32},{48,40},{56,48},{64,56},{72,6... | collective-permute-start | bytes 5048 | tf_op jit(solution)/shard_map/ppermute | solution.py:17
  36.5 24.5 %collective-permute-start.1 = (f32[1,42,10,1]{3,0,2,1:T(1,128)S(1)}, f32[1,42,10,1]{3,0,2,1:T(1,128)S(1)}, u32[]{:S(2)}, u32[]{:S(2)}) collective-permute-start(f32[1,42,10,1]{3,0,2,1:T(1,128)S(1)} %get-tuple-element.57), channel_id=1, source_target_pairs={{0,8},{8,16},{16,24},{24,32},{32,40},{40,48},{48,56},{56,64},{64,7... | collective-permute-start | bytes 5048 | tf_op jit(solution)/shard_map/ppermute | solution.py:16
  67.0 2.5 copy-start.2
  69.5 1.2 copy-start.5
  71.5 5.5 %copy-start.6 = (f32[512,4]{0,1:T(4,128)S(1)}, f32[512,4]{0,1:T(4,128)}, u32[]{:S(2)}) copy-start(f32[512,4]{0,1:T(4,128)} %param.17) | copy-start | bytes 24580
  72.1 7.0 %collective-permute-start.2 = (f32[1,42,10,1]{3,0,2,1:T(1,128)S(1)}, f32[1,42,10,1]{3,0,2,1:T(1,128)S(1)}, u32[]{:S(2)}, u32[]{:S(2)}) collective-permute-start(f32[1,42,10,1]{3,0,2,1:T(1,128)S(1)} %get-tuple-element.52), channel_id=1, source_target_pairs={{8,0},{16,8},{24,16},{32,24},{40,32},{48,40},{56,48},{64,56},{72,6... | collective-permute-start | bytes 5048 | tf_op jit(solution)/shard_map/ppermute | solution.py:17
  74.0 23.4 %collective-permute-start.3 = (f32[1,42,10,1]{3,0,2,1:T(1,128)S(1)}, f32[1,42,10,1]{3,0,2,1:T(1,128)S(1)}, u32[]{:S(2)}, u32[]{:S(2)}) collective-permute-start(f32[1,42,10,1]{3,0,2,1:T(1,128)S(1)} %get-tuple-element.53), channel_id=1, source_target_pairs={{0,8},{8,16},{16,24},{24,32},{32,40},{40,48},{48,56},{56,64},{64,7... | collective-permute-start | bytes 5048 | tf_op jit(solution)/shard_map/ppermute | solution.py:16
  107.7 320.2 %copy-start.8 = (s32[512]{0:T(512)S(1)}, s32[512]{0:T(512)}, u32[]{:S(2)}) copy-start(s32[512]{0:T(512)} %param.19) | copy-start | bytes 6148
  108.0 319.9 %copy-start.1 = (f32[1,42,10,512]{3,2,1,0:T(8,128)}, f32[1,42,10,512]{3,2,1,0:T(8,128)S(1)}, u32[]{:S(2)}) copy-start(f32[1,42,10,512]{3,2,1,0:T(8,128)S(1)} %copy_select_fusion) | copy-start | bytes 2580484
  426.6 11.9 %collective-permute-start.4 = (f32[4,16384]{1,0:T(4,128)S(1)}, f32[4,16384]{1,0:T(4,128)S(1)}, u32[]{:S(2)}, u32[]{:S(2)}) collective-permute-start(f32[4,16384]{1,0:T(4,128)S(1)} %all_gather.3), channel_id=1, source_target_pairs={{0,512},{256,768},{1,513},{257,769},{2,514},{258,770},{3,515},{259... | collective-permute-start | bytes 786440 | tf_op jit(solution)/shard_map/ppermute | solution.py:25
  452.4 3.7 slice-start
Sparse Core Ops, SparseCore 0:
  109.3 226.7 all-reduce.2
where the time goes:
time: 465 us; the launch traced here: 464 us
  waiting for transfers between devices  278 us (60%)
  blocking collectives  89.8 us (19%)
  starting transfers between devices  33.6 us (7%)
  other arithmetic  24.6 us (5%)
  local copies, waits for them, and re-layouts  22.6 us (5%)
  between operations  15.2 us (3%)
    unnamed x2, waiting for transfers between devices  227 us
    all_gather x1, blocking collectives, body(): whole = lax.all_gather(surface, 'tile', axis=1, tiled=True)  89.8 us
    ppermute x2, waiting for transfers between devices, extended(): before = lax.ppermute(last, axis, up)  39.5 us
    ppermute x2, starting transfers between devices, extended(): after = lax.ppermute(first, axis, down)  27.8 us
    concatenate x2, other arithmetic, extended(): x = jnp.concatenate([before, x, after], axis=dim)  12.1 us
    ppermute x1, waiting for transfers between devices, passed_along(): lax.ppermute(value, axis, [(source, source + steps) for source in range(f...  9.8 us
  transfers between devices with their start and end apart: 6, of which 5 were waited for; matrix products, arithmetic and copies ran while one was open for 1% of the time, Pallas kernels for 0%

commit v1 on v0

v1 whole, which is shorter than its diff:
```python
import functools

import jax
import jax.numpy as jnp
from jax import lax
from jax.experimental import pallas as pl
from jax.experimental.pallas import tpu as pltpu
from jax.sharding import PartitionSpec as P

MESH = pl.DeviceIdType.MESH
F32 = jnp.float32
HIGHEST = lax.Precision.HIGHEST


def dot(a, b):
    return jnp.dot(a, b, precision=HIGHEST, preferred_element_type=F32)


def flux(q, up, un):
    n = q.shape[1]
    return up * q + un * pltpu.roll(q, n - 1, 1)


def tracer_step(q, up, un):
    f = flux(q, up, un)
    return q - (f - pltpu.roll(f, 1, 1))


def heat_step(t, up, un, d):
    n = t.shape[1]
    f = flux(t, up, un)
    return t + (
        -(f - pltpu.roll(f, 1, 1)) + d * (pltpu.roll(t, 1, 1) - 2.0 * t + pltpu.roll(t, n - 1, 1))
    )


def kernel(
    t_hbm, u_hbm, d_hbm, q_hbm, m_ref, w_hbm, i_hbm, sea_hbm,
    tout_hbm, qout_hbm,
    t40, u40, d40, qin, qout, w_v, i_v, i_s, sea_v,
    ext, coef, sendA, sendB, haloA, haloB, gath, flip_s, flip_r, own, srow, piece, rows, pieces, out40,
    in_sem, q_sem, sA, rA, sB, rB, sX, rX, sF, rF, sR, rR, sP, rP, o_sem,
):
    comp, tile, lev = lax.axis_index("comp"), lax.axis_index("tile"), lax.axis_index("lev")
    tiles = lax.axis_size("tile")
    half, x = lev // 4, lax.rem(lev, 4)
    is_sky = comp < 2
    is_target = jnp.logical_and(comp >= 2, lev == 0)
    left, right = lax.rem(tile + tiles - 1, tiles), lax.rem(tile + 1, tiles)
    x_peers = [half * 4 + lax.rem(x + k, 4) for k in range(1, 4)]
    other = lax.rem(lev + 4, 8)

    loads = [
        pltpu.make_async_copy(t_hbm, t40, in_sem.at[0]),
        pltpu.make_async_copy(u_hbm, u40, in_sem.at[1]),
        pltpu.make_async_copy(d_hbm, d40, in_sem.at[2]),
        pltpu.make_async_copy(q_hbm, qin, q_sem),
        pltpu.make_async_copy(w_hbm, w_v, in_sem.at[3]),
        pltpu.make_async_copy(i_hbm, i_v, in_sem.at[4]),
        pltpu.make_async_copy(i_hbm, i_s, in_sem.at[5]),
        pltpu.make_async_copy(sea_hbm, sea_v, in_sem.at[6]),
    ]
    for c in loads:
        c.start()

    bar = pltpu.get_barrier_semaphore()

    def hello(**where):
        pl.semaphore_signal(bar, inc=1, device_id=where, device_id_type=MESH)

    hello(tile=left)
    hello(tile=right)
    for p in x_peers:
        hello(lev=p)
    hello(lev=other)

    @pl.when(is_target)
    def _():
        def body(k, _):
            for j in range(8):
                hello(comp=comp - 2, tile=lax.rem(tile + k, tiles), lev=j)
            return 0

        lax.fori_loop(0, tiles, body, 0)

    def iota(shape, dim):
        return lax.broadcasted_iota(jnp.int32, shape, dim)

    i, j = iota((48, 80), 0), iota((48, 80), 1)
    wanted = jnp.where(i < 16, lev * 10 + i, jnp.where(i < 32, other * 10 + i - 16, i - 32))
    used = jnp.where(i < 16, i, jnp.where(i < 32, i - 16, i - 23)) < 10
    pick_rows = jnp.where(jnp.logical_and(used, wanted == j), 1.0, 0.0).astype(F32)
    i, j = iota((80, 64), 0), iota((80, 64), 1)
    r = lax.rem(j, 16)
    pick_cols = jnp.where(
        jnp.logical_and(r < 10, i == half * 40 + (j // 16) * 10 + r), 1.0, 0.0
    ).astype(F32)
    matrix = dot(dot(pick_rows, m_ref[...]), pick_cols)

    lane = iota((16, 128), 1)
    row = iota((16, 128), 0)

    for c in loads[:3]:
        c.wait()
    blank = jnp.zeros((16, 640), F32)
    for k in range(3):
        ext[k] = blank
    for k, ref in enumerate((t40, u40, d40)):
        for c in range(4):
            ext[k, 0:10, c * 128 : (c + 1) * 128] = ref[pl.ds(c, 10, stride=4), :]
    ends = [ext[k, :, 384:512] for k in range(3)]
    starts = [ext[k, :, 0:128] for k in range(3)]
    sendA[0] = jnp.where(
        lane >= 124, ends[0], jnp.where(lane >= 120, pltpu.roll(ends[1], 124, 1), pltpu.roll(ends[2], 120, 1))
    )
    sendA[1] = jnp.where(
        lane < 4, starts[0], jnp.where(lane < 8, pltpu.roll(starts[1], 4, 1), pltpu.roll(starts[2], 8, 1))
    )
    loads[3].wait()
    lane40 = iota((40, 128), 1)

    def pack(r, carry):
        to_right, to_left = carry
        mine = jnp.logical_and(lane40 >= 2 * r, lane40 < 2 * r + 2)
        to_right = jnp.where(mine, pltpu.roll(qin[r, :, 384:512], 2 * r + 2, 1), to_right)
        to_left = jnp.where(mine, pltpu.roll(qin[r, :, 0:128], 2 * r, 1), to_left)
        return to_right, to_left

    zero40 = jnp.zeros((40, 128), F32)
    to_right, to_left = lax.fori_loop(0, 10, pack, (zero40, zero40))
    sendB[0] = to_right
    sendB[1] = to_left

    pl.semaphore_wait(bar, 6 + jnp.where(is_sky, tiles, 0))

    def send(src, dst, s, r, **where):
        c = pltpu.make_async_remote_copy(
            src_ref=src, dst_ref=dst, send_sem=s, recv_sem=r, device_id=where, device_id_type=MESH
        )
        c.start()
        return c

    edges = [
        send(sendA.at[0], haloA.at[0], sA.at[0], rA.at[0], tile=right),
        send(sendA.at[1], haloA.at[1], sA.at[1], rA.at[1], tile=left),
        send(sendB.at[0], haloB.at[0], sB.at[0], rB.at[0], tile=right),
        send(sendB.at[1], haloB.at[1], sB.at[1], rB.at[1], tile=left),
    ]
    for c in edges:
        c.wait()
    from_left, from_right = haloA[0], haloA[1]
    low = lane < 64
    ext[0, :, 512:640] = jnp.where(low, from_right, from_left)
    ext[1, :, 512:640] = jnp.where(low, pltpu.roll(from_right, 124, 1), pltpu.roll(from_left, 4, 1))
    ext[2, :, 512:640] = jnp.where(low, pltpu.roll(from_right, 120, 1), pltpu.roll(from_left, 8, 1))
    sky = jnp.where(is_sky, 1.0, 0.0).astype(F32)
    up, un = jnp.maximum(ext[1], 0.0), jnp.minimum(ext[1], 0.0)
    coef[0] = up
    coef[1] = un
    coef[2] = up * sky
    coef[3] = un * sky
    heat = heat_step(ext[0], up, un, ext[2])
    heat = heat_step(heat, up * sky, un * sky, ext[2] * sky)[:, 0:512]

    low40 = lane40 < 64

    def level(r):
        edge = jnp.where(
            low40,
            pltpu.roll(haloB[1], lax.rem(128 - 2 * r, 128), 1),
            pltpu.roll(haloB[0], 126 - 2 * r, 1),
        )
        q = jnp.concatenate([qin[r], edge], axis=1)
        up, un, up2, un2 = (jnp.broadcast_to(coef[k, pl.ds(r, 1), :], (40, 640)) for k in range(4))
        q = tracer_step(tracer_step(q, up, un), up2, un2)
        qout[r] = q[:, 0:512]

    level(0)
    row8 = iota((8, 512), 0)
    rows_q = pltpu.roll(qout[0, 0:8, :], 2, 0)
    gath[x, 0:8, :] = heat[0:8]
    gath[x, 8:16, :] = jnp.where(row8 < 2, heat[8:16], jnp.where(row8 < 5, rows_q, 0.0))
    shares = [send(gath.at[x], gath.at[x], sX.at[k], rX.at[k], lev=x_peers[k]) for k in range(3)]
    for c in shares:
        c.wait()
    product = dot(matrix, jnp.concatenate([gath[k] for k in range(4)], axis=0))
    own[...] = product[0:16]
    for c in range(4):
        flip_s[pl.ds(c, 10, stride=4), :] = product[16:26, c * 128 : (c + 1) * 128]
    top = product[32:33, :]
    line = jnp.where(
        x == 0, gath[0, 10:11, :], jnp.where(x == 1, gath[0, 11:12, :], jnp.where(x == 2, gath[0, 12:13, :], top))
    )
    for c in range(4):
        srow[c : c + 1, :] = line[:, c * 128 : (c + 1) * 128]
    piece[...] = jnp.where(
        x == 0, top[:, 0:128], jnp.where(x == 1, top[:, 128:256], jnp.where(x == 2, top[:, 256:384], top[:, 384:512]))
    )

    flip = send(flip_s, flip_r, sF, rF, lev=other)

    @pl.when(jnp.logical_and(is_sky, half == 0))
    def _():
        def body(k, _):
            send(srow, rows.at[x, tile], sR, rR, comp=comp + 2, tile=lax.rem(tile + k, tiles), lev=0)
            return 0

        lax.fori_loop(0, tiles, body, 0)

    @pl.when(jnp.logical_and(is_sky, half == 1))
    def _():
        def body(k, _):
            send(piece, pieces.at[x, tile], sP, rP, comp=comp + 2, tile=lax.rem(tile + k, tiles), lev=0)
            return 0

        lax.fori_loop(0, tiles, body, 0)

    def more(r, _):
        level(r)
        pltpu.make_async_copy(qout.at[r], qout_hbm.at[r], o_sem.at[0]).start()
        return 0

    lax.fori_loop(1, 10, more, 0)

    flip.wait()
    for c in range(4):
        out40[pl.ds(c, 10, stride=4), :] = own[0:10, c * 128 : (c + 1) * 128] + flip_r[pl.ds(c, 10, stride=4), :]

    for c in loads[4:]:
        c.wait()

    @pl.when(is_target)
    def _():
        pltpu.make_async_copy(rows, rows, rR).wait()
        pltpu.make_async_copy(pieces, pieces, rP).wait()
        block = lax.shift_right_logical(i_s[0, 256], 9)
        before, after = lax.rem(block + tiles - 1, tiles), lax.rem(block + 1, tiles)
        window = []
        for f in range(4):
            b, m, a = rows[f, before], rows[f, block], rows[f, after]
            window.append([b[3:4]] + [m[c : c + 1] for c in range(4)] + [a[0:1]])
        extra = [pieces[3, before]] + [pieces[c, block] for c in range(4)] + [pieces[0, after]]
        window[3] = [a + b for a, b in zip(window[3], extra)]
        for c in range(4):
            at = slice(c * 128, (c + 1) * 128)
            place = jnp.bitwise_and(i_v[:, at] - block * 512 + 128, tiles * 512 - 1)
            place = jnp.concatenate([place, place], axis=0)
            which, within = lax.shift_right_logical(place, 7), jnp.bitwise_and(place, 127)
            weight = w_v[:, at]
            sea = sea_v[c : c + 1, :] == 1
            for pair in ((0, 1), (2, 3)):
                got = jnp.zeros((8, 128), F32)
                for m in range(c, c + 3):
                    source = jnp.concatenate(
                        [jnp.broadcast_to(window[f][m], (4, 128)) for f in pair], axis=0
                    )
                    taken = jnp.take_along_axis(source, within, axis=1, mode="promise_in_bounds")
                    got = jnp.where(which == m, taken, got)
                for k, f in enumerate(pair):
                    remapped = jnp.sum(got[4 * k : 4 * k + 4] * weight, axis=0, keepdims=True)
                    if f < 3:
                        s = qout[0, f : f + 1, at]
                        qout[0, f : f + 1, at] = jnp.where(sea, s + 0.5 * (remapped - s), s)
                    else:
                        s = out40[c : c + 1, :]
                        out40[c : c + 1, :] = jnp.where(sea, s + 0.5 * (remapped - s), s)

    last = [
        pltpu.make_async_copy(out40, tout_hbm, o_sem.at[1]),
        pltpu.make_async_copy(qout.at[0], qout_hbm.at[0], o_sem.at[2]),
    ]
    for c in last:
        c.start()

    @pl.when(jnp.logical_and(is_sky, half == 0))
    def _():
        pltpu.make_async_copy(rows.at[0], rows.at[0], sR).wait()

    @pl.when(jnp.logical_and(is_sky, half == 1))
    def _():
        pltpu.make_async_copy(pieces.at[0], pieces.at[0], sP).wait()

    pltpu.make_async_copy(qout.at[pl.ds(1, 9)], qout_hbm.at[pl.ds(1, 9)], o_sem.at[0]).wait()
    for c in last:
        c.wait()


def body(t, u, q, d, m, w, i, sea):
    any_ = pl.BlockSpec(memory_space=pl.ANY)
    vmem = pl.BlockSpec(memory_space=pltpu.VMEM)
    dma = pltpu.SemaphoreType.DMA
    tiles = lax.axis_size("tile")
    buf = lambda *s: pltpu.VMEM(s, F32)
    tout, qout = pl.pallas_call(
        kernel,
        out_shape=(jax.ShapeDtypeStruct((40, 128), F32), jax.ShapeDtypeStruct((10, 40, 512), F32)),
        in_specs=[any_, any_, any_, any_, vmem, any_, any_, any_],
        out_specs=(any_, any_),
        scratch_shapes=[
            buf(40, 128), buf(40, 128), buf(40, 128), buf(10, 40, 512), buf(10, 40, 512),
            buf(4, 512), pltpu.VMEM((4, 512), jnp.int32), pltpu.SMEM((4, 512), jnp.int32), pltpu.VMEM((4, 128), jnp.int32),
            buf(3, 16, 640), buf(4, 16, 640), buf(2, 16, 128), buf(2, 40, 128), buf(2, 16, 128), buf(2, 40, 128),
            buf(4, 16, 512), buf(40, 128), buf(40, 128), buf(16, 512), buf(4, 128), buf(1, 128),
            buf(4, tiles, 4, 128), buf(4, tiles, 1, 128), buf(40, 128),
            dma((7,)), dma, dma((2,)), dma((2,)), dma((2,)), dma((2,)), dma((3,)), dma((3,)), dma, dma,
            dma, dma, dma, dma, dma((3,)),
        ],
        compiler_params=pltpu.CompilerParams(
            collective_id=0, has_side_effects=True, vmem_limit_bytes=24 * 1024 * 1024
        ),
    )(
        t.reshape(40, 128), u.reshape(40, 128), d.reshape(40, 128), jnp.transpose(q[0], (1, 0, 2)),
        m[0], w.T, i.T, sea.reshape(4, 128),
    )
    return tout.reshape(1, 10, 512), jnp.transpose(qout, (1, 0, 2))[None]


def solution(mesh):
    in_specs = (
        P("comp", "lev", "tile"),
        P("comp", "lev", "tile"),
        P("comp", None, "lev", "tile"),
        P("comp", "lev", "tile"),
        P("comp", None, None),
        P("tile", None),
        P("tile", None),
        P("tile"),
    )
    out_specs = (P("comp", "lev", "tile"), P("comp", None, "lev", "tile"))
    return jax.shard_map(body, mesh=mesh, in_specs=in_specs, out_specs=out_specs, check_vma=False)
```

time: 465 us -> 67 us (0.14)
  waiting for transfers between devices: 278 us -> 0 us
  blocking collectives: 89.8 us -> 0 us
  Pallas kernels: 0 us -> 58.8 us
  starting transfers between devices: 33.6 us -> 0 us
  other arithmetic: 24.6 us -> 0 us
  local copies, waits for them, and re-layouts: 22.6 us -> 6.98 us
  between operations: 15.2 us -> 0.66 us
    unnamed x2 -> x0, waiting for transfers between devices: 227 us -> none
    all_gather x1 -> x0, blocking collectives: 89.8 us -> none  [body(): whole = lax.all_gather(surface, 'tile', axis=1, tiled=True)]
    pallas_call x0 -> x1, Pallas kernels: none -> 58.8 us  [body(): pl.pallas_call(kernel, out_shape=(jax.ShapeDtypeStruct((40, 128), F32), j...]
    ppermute x5 -> x0, waiting for transfers between devices: 50.7 us -> none  [the longest x2 39.5 us: extended(): before = lax.ppermute(last, axis, up)]
    ppermute x5 -> x0, starting transfers between devices: 33.6 us -> none  [the longest x2 27.8 us: extended(): after = lax.ppermute(first, axis, down)]
    concatenate x7 -> x0, other arithmetic: 14.4 us -> none  [the longest x2 12.1 us: extended(): x = jnp.concatenate([before, x, after], axis=dim)]
    gather x1 -> x0, local copies, waits for them, and re-layouts: 8.85 us -> none  [body(): picked = received[:, sky_point_of_entry]]
    ppermute x1 -> x0, local copies, waits for them, and re-layouts: 5.03 us -> none  [passed_along(): lax.ppermute(value, axis, [(source, source + steps) for source in range(f...]
  transfers between devices with their start and end apart: 6 -> 0, of which waited for: 5 -> 0; matrix products, arithmetic and copies ran while one was open for 1% -> 0% of each run, Pallas kernels for 0% -> 0%
where the time goes in v1:
time: 67 us; the launch traced here: 66.5 us
  Pallas kernels  58.8 us (88%)
  local copies, waits for them, and re-layouts  6.98 us (10%)
    pallas_call x1, Pallas kernels, body(): pl.pallas_call(kernel, out_shape=(jax.ShapeDtypeStruct((40, 128), F32), j...  58.8 us
    unnamed x18, local copies, waits for them, and re-layouts  6.98 us

profile of v1, /device:TPU:24, one launch (start us, length us, event | category | flops | bytes accessed | tf_op | source)
XLA Modules:
  0.0 66.5 jit_solution(9279207012821834701)
XLA Ops:
  0.6 0.0 copy-start.5
  0.6 0.0 copy-start.7
  0.7 0.7 %copy-done.5 = f32[512,4]{0,1:T(4,128)S(1)} copy-done((f32[512,4]{0,1:T(4,128)S(1)}, f32[512,4]{0,1:T(4,128)}, u32[]{:S(2)}) %copy-start.5) | copy-done | bytes 8216
  1.3 0.0 copy-done.7
  1.3 0.0 copy-start
  1.3 1.1 %copy-done = f32[1,40,10,512]{3,1,2,0:T(8,128)S(1)} copy-done((f32[1,40,10,512]{3,1,2,0:T(8,128)S(1)}, f32[1,40,10,512]{3,1,2,0:T(8,128)}, u32[]{:S(2)}) %copy-start) | copy-done | bytes 819224
  2.5 0.0 copy-start.1
  2.5 0.8 %copy-done.1 = f32[1,80,80]{2,1,0:T(8,128)S(1)} copy-done((f32[1,80,80]{2,1,0:T(8,128)S(1)}, f32[1,80,80]{2,1,0:T(8,128)}, u32[]{:S(2)}) %copy-start.1) | copy-done | bytes 25624
  3.3 0.0 copy-start.2
  3.3 0.7 %copy-done.2 = f32[1,10,512]{2,0,1:T(1,128)S(1)} copy-done((f32[1,10,512]{2,0,1:T(1,128)S(1)}, f32[1,10,512]{2,0,1:T(1,128)}, u32[]{:S(2)}) %copy-start.2) | copy-done | bytes 20504
  4.0 0.0 copy-start.3
  4.0 0.7 %copy-done.3 = f32[1,10,512]{2,0,1:T(1,128)S(1)} copy-done((f32[1,10,512]{2,0,1:T(1,128)S(1)}, f32[1,10,512]{2,0,1:T(1,128)}, u32[]{:S(2)}) %copy-start.3) | copy-done | bytes 20504
  4.7 0.0 copy-start.4
  4.7 0.7 %copy-done.4 = f32[1,10,512]{2,0,1:T(1,128)S(1)} copy-done((f32[1,10,512]{2,0,1:T(1,128)S(1)}, f32[1,10,512]{2,0,1:T(1,128)}, u32[]{:S(2)}) %copy-start.4) | copy-done | bytes 20504
  5.4 0.0 copy-start.6
  5.4 0.7 %copy-done.6 = s32[512,4]{0,1:T(4,128)S(1)} copy-done((s32[512,4]{0,1:T(4,128)S(1)}, s32[512,4]{0,1:T(4,128)}, u32[]{:S(2)}) %copy-start.6) | copy-done | bytes 8216
  6.1 58.8 %shard_map.95 = (f32[40,128]{1,0:T(8,128)S(1)}, f32[10,40,512]{2,1,0:T(8,128)S(1)}) custom-call(f32[40,128]{1,0:T(8,128)S(1)} %bitcast.18, f32[40,128]{1,0:T(8,128)S(1)} %bitcast.19, f32[40,128]{1,0:T(8,128)S(1)} %bitcast.20, f32[10,40,512]{2,1,0:T(8,128)S(1)} %bitcast.14, f32[80,80]{1,0:T(8,128)S(1)} %bitcast.16, f32[4,512]{1,0:T(4,128)S(1)} %bitcast.21, ...), custom_call_target="tpu_custom_call" | custom-call | tf_op jit(solution)/shard_map/pallas_call | solution.py:294
  65.0 0.6 copy.14
  65.6 0.9 %copy.15 = f32[1,40,10,512]{3,1,2,0:T(8,128)} copy(f32[1,40,10,512]{3,1,2,0:T(8,128)S(1)} %bitcast.15) | data formatting | bytes 1638400
Async XLA Ops:
  0.6 0.7 %copy-start.5 = (f32[512,4]{0,1:T(4,128)S(1)}, f32[512,4]{0,1:T(4,128)}, u32[]{:S(2)}) copy-start(f32[512,4]{0,1:T(4,128)} %param.13) | copy-start | bytes 24580
  0.6 0.7 %copy-start.7 = (s32[512]{0:T(512)S(1)}, s32[512]{0:T(512)}, u32[]{:S(2)}) copy-start(s32[512]{0:T(512)} %param.15) | copy-start | bytes 6148
  1.3 1.1 %copy-start = (f32[1,40,10,512]{3,1,2,0:T(8,128)S(1)}, f32[1,40,10,512]{3,1,2,0:T(8,128)}, u32[]{:S(2)}) copy-start(f32[1,40,10,512]{3,1,2,0:T(8,128)} %param.10) | copy-start | bytes 2457604
  2.5 0.8 %copy-start.1 = (f32[1,80,80]{2,1,0:T(8,128)S(1)}, f32[1,80,80]{2,1,0:T(8,128)}, u32[]{:S(2)}) copy-start(f32[1,80,80]{2,1,0:T(8,128)} %param.12) | copy-start | bytes 76804
  3.3 0.7 %copy-start.2 = (f32[1,10,512]{2,0,1:T(1,128)S(1)}, f32[1,10,512]{2,0,1:T(1,128)}, u32[]{:S(2)}) copy-start(f32[1,10,512]{2,0,1:T(1,128)} %param.8) | copy-start | bytes 61444
  4.0 0.7 %copy-start.3 = (f32[1,10,512]{2,0,1:T(1,128)S(1)}, f32[1,10,512]{2,0,1:T(1,128)}, u32[]{:S(2)}) copy-start(f32[1,10,512]{2,0,1:T(1,128)} %param.9) | copy-start | bytes 61444
  4.7 0.7 %copy-start.4 = (f32[1,10,512]{2,0,1:T(1,128)S(1)}, f32[1,10,512]{2,0,1:T(1,128)}, u32[]{:S(2)}) copy-start(f32[1,10,512]{2,0,1:T(1,128)} %param.11) | copy-start | bytes 61444
  5.4 0.7 %copy-start.6 = (s32[512,4]{0,1:T(4,128)S(1)}, s32[512,4]{0,1:T(4,128)}, u32[]{:S(2)}) copy-start(s32[512,4]{0,1:T(4,128)} %param.14) | copy-start | bytes 24580

commit v2 on v1

v2 whole, which is shorter than its diff:
```python
import functools

import jax
import jax.numpy as jnp
from jax import lax
from jax.experimental import pallas as pl
from jax.experimental.pallas import tpu as pltpu
from jax.sharding import PartitionSpec as P

MESH = pl.DeviceIdType.MESH
F32 = jnp.float32
HIGHEST = lax.Precision.HIGHEST


def dot(a, b):
    return jnp.dot(a, b, precision=HIGHEST, preferred_element_type=F32)


def flux(q, up, un):
    n = q.shape[1]
    return up * q + un * pltpu.roll(q, n - 1, 1)


def tracer_step(q, up, un):
    f = flux(q, up, un)
    return q - (f - pltpu.roll(f, 1, 1))


def heat_step(t, up, un, d):
    n = t.shape[1]
    f = flux(t, up, un)
    return t + (
        -(f - pltpu.roll(f, 1, 1)) + d * (pltpu.roll(t, 1, 1) - 2.0 * t + pltpu.roll(t, n - 1, 1))
    )


def drain(ref, sem):
    pltpu.make_async_copy(ref, ref, sem).wait()


def send(src, dst, s, r, **where):
    pltpu.make_async_remote_copy(
        src_ref=src, dst_ref=dst, send_sem=s, recv_sem=r, device_id=where, device_id_type=MESH
    ).start()


def iota(shape, dim):
    return lax.broadcasted_iota(jnp.int32, shape, dim)


def joined(from_right, from_left):
    low = iota((16, 128), 1) < 64
    return (
        jnp.where(low, from_right, from_left),
        jnp.where(low, pltpu.roll(from_right, 124, 1), pltpu.roll(from_left, 4, 1)),
        jnp.where(low, pltpu.roll(from_right, 120, 1), pltpu.roll(from_left, 8, 1)),
    )


def courant(u):
    return jnp.maximum(u, 0.0), jnp.minimum(u, 0.0)


def kernel(
    t_hbm, u_hbm, d_hbm, q_hbm, m_hbm, w_hbm, i_hbm, sea_hbm,
    tout, qout,
    t40, u40, d40, qin, m_v, w_v, i_v, i_s, sea_v,
    ext, coef, sendA, sendB, haloA, haloB, gath, flip_s, flip_r, own, srow, piece, rows, pieces,
    ring, ring_coef, wrapB, edge_s, edge_r, edge_rows,
    in_sem, sA, rA, sB, rB, sX, rX, sF, rF, sR, rR, sP, rP, sE, rE, sW, rW, sG, rG, ready,
):
    comp, tile, lev = lax.axis_index("comp"), lax.axis_index("tile"), lax.axis_index("lev")
    tiles = lax.axis_size("tile")
    half, x = lev // 4, lax.rem(lev, 4)
    is_sky = comp < 2
    is_target = jnp.logical_and(comp >= 2, lev == 0)
    first, last = tile == 0, tile == tiles - 1
    is_wrap = jnp.logical_or(first, last)
    order = half * 2 + jnp.where(last, 1, 0)
    x_peers = [half * 4 + lax.rem(x + k, 4) for k in range(1, 4)]
    other = lax.rem(lev + 4, 8)

    def group(g, k):
        return {"tile": (tiles - 1) * (g % 2), "lev": (g // 2) * 4 + k}

    pairs = (
        (t_hbm, t40), (u_hbm, u40), (d_hbm, d40), (q_hbm, qin), (m_hbm, m_v),
        (w_hbm, w_v), (i_hbm, i_v), (i_hbm, i_s), (sea_hbm, sea_v),
    )
    loads = [pltpu.make_async_copy(a, b, in_sem.at[k]) for k, (a, b) in enumerate(pairs)]
    for c in loads:
        c.start()

    bar = pltpu.get_barrier_semaphore()

    def hello(**where):
        pl.semaphore_signal(bar, inc=1, device_id=where, device_id_type=MESH)

    @pl.when(tile > 0)
    def _():
        hello(tile=tile - 1)

    @pl.when(tile < tiles - 1)
    def _():
        hello(tile=tile + 1)

    for p in x_peers:
        hello(lev=p)

    @pl.when(half == 0)
    def _():
        hello(lev=lev + 4)

    @pl.when(is_wrap)
    def _():
        for g in range(1, 4):

            @pl.when(g > order)
            def _():
                for k in range(4):
                    hello(**group(g, k))

    @pl.when(is_target)
    def _():
        def body(k, _):
            for j in range(8):
                hello(comp=comp - 2, tile=lax.rem(tile + k, tiles), lev=j)
            return 0

        lax.fori_loop(0, tiles, body, 0)

    lane = iota((16, 128), 1)

    blank = jnp.zeros((16, 640), F32)
    for k in range(3):
        ext[k] = blank
    for c in loads[:3]:
        c.wait()
    for k, ref in enumerate((t40, u40, d40)):
        for c in range(4):
            ext[k, 0:10, c * 128 : (c + 1) * 128] = ref[pl.ds(c, 10, stride=4), :]
    ends = [ext[k, :, 384:512] for k in range(3)]
    starts = [ext[k, :, 0:128] for k in range(3)]
    sendA[0] = jnp.where(
        lane >= 124, ends[0], jnp.where(lane >= 120, pltpu.roll(ends[1], 124, 1), pltpu.roll(ends[2], 120, 1))
    )
    sendA[1] = jnp.where(
        lane < 4, starts[0], jnp.where(lane < 8, pltpu.roll(starts[1], 4, 1), pltpu.roll(starts[2], 8, 1))
    )
    loads[3].wait()
    lane40 = iota((40, 128), 1)
    low40 = lane40 < 64
    zero40 = jnp.zeros((40, 128), F32)

    def pack(r, carry):
        to_right, to_left = carry
        mine = jnp.logical_and(lane40 >= 2 * r, lane40 < 2 * r + 2)
        to_right = jnp.where(mine, pltpu.roll(qin[r, :, 384:512], 2 * r + 2, 1), to_right)
        to_left = jnp.where(mine, pltpu.roll(qin[r, :, 0:128], 2 * r, 1), to_left)
        return to_right, to_left

    to_right, to_left = lax.fori_loop(0, 10, pack, (zero40, zero40))
    sendB[0] = to_right
    sendB[1] = to_left

    @pl.when(first)
    def _():
        haloA[0] = jnp.zeros((16, 128), F32)
        haloB[0] = zero40

    @pl.when(last)
    def _():
        haloA[1] = jnp.zeros((16, 128), F32)
        haloB[1] = zero40

    greeted = (
        jnp.where(tile > 0, 1, 0) + jnp.where(tile < tiles - 1, 1, 0) + 3 + half
        + jnp.where(is_sky, tiles, 0) + jnp.where(is_wrap, 4 * order, 0)
    )
    pl.semaphore_wait(bar, greeted)

    @pl.when(tile < tiles - 1)
    def _():
        send(sendA.at[0], haloA.at[0], sA.at[0], rA.at[0], tile=tile + 1)
        send(sendB.at[0], haloB.at[0], sB.at[0], rB.at[0], tile=tile + 1)

    @pl.when(tile > 0)
    def _():
        send(sendA.at[1], haloA.at[1], sA.at[1], rA.at[1], tile=tile - 1)
        send(sendB.at[1], haloB.at[1], sB.at[1], rB.at[1], tile=tile - 1)

    @pl.when(half == 1)
    def _():
        pl.semaphore_signal(ready, inc=1, device_id={"lev": lev - 4}, device_id_type=MESH)

    loads[4].wait()
    i, j = iota((48, 80), 0), iota((48, 80), 1)
    wanted = jnp.where(i < 16, lev * 10 + i, jnp.where(i < 32, other * 10 + i - 16, i - 32))
    used = jnp.where(i < 16, i, jnp.where(i < 32, i - 16, i - 23)) < 10
    pick_rows = jnp.where(jnp.logical_and(used, wanted == j), 1.0, 0.0).astype(F32)

    def pick_cols(count, start):
        i, j = iota((80, count), 0), iota((80, count), 1)
        r = lax.rem(j, 16)
        return jnp.where(jnp.logical_and(r < 10, i == start + (j // 16) * 10 + r), 1.0, 0.0).astype(F32)

    @pl.when(is_wrap)
    def _():
        ring[order, x] = jnp.where(last, sendA[0], sendA[1])
        mine = ring.at[order, x]
        for p in x_peers:
            send(mine, mine, sE.at[order], rE.at[order], lev=p)
        for g in range(0, 3):

            @pl.when(g < order)
            def _():
                for k in range(4):
                    send(mine, mine, sE.at[g], rE.at[order], **group(g, k))

        @pl.when(last)
        def _():
            send(sendB.at[0], wrapB, sW, rW, tile=0)

        @pl.when(is_sky)
        def _():
            i, j = iota((16, 80), 0), iota((16, 80), 1)
            here = jnp.logical_and(i < 10, j == lev * 10 + i)
            scale = jnp.sum(jnp.where(here, jnp.broadcast_to(m_v[0:1, :], (16, 80)), 0.0), axis=1, keepdims=True)
            is_t = jnp.where(last, lane - 124, 3 - lane) >= 0
            edge = ring[order, x]
            edge = jnp.where(is_t, edge * scale, edge)
            q3 = jnp.where(last, qin[0, 0:8, 384:512], qin[0, 0:8, 0:128])
            low8 = iota((8, 128), 0) < 2
            edge_s[0:8] = edge[0:8]
            edge_s[8:16] = jnp.where(low8, edge[8:16], pltpu.roll(q3, 2, 0))
            side = jnp.where(last, 1, 0)

            def body(k, _):
                send(edge_s, edge_r.at[side, lev], sG, rG, comp=comp + 2, tile=lax.rem(tile + k, tiles), lev=0)
                return 0

            lax.fori_loop(0, tiles, body, 0)

    matrix = dot(dot(pick_rows, m_v[...]), pick_cols(64, half * 40))

    @pl.when(tile > 0)
    def _():
        drain(haloA.at[0], rA.at[0])
        drain(haloB.at[0], rB.at[0])

    @pl.when(tile < tiles - 1)
    def _():
        drain(haloA.at[1], rA.at[1])
        drain(haloB.at[1], rB.at[1])

    for k, block in enumerate(joined(haloA[1], haloA[0])):
        ext[k, :, 512:640] = block
    sky = jnp.where(is_sky, 1.0, 0.0).astype(F32)
    up, un = courant(ext[1])
    coef[0] = up
    coef[1] = un
    coef[2] = up * sky
    coef[3] = un * sky
    heat = heat_step(ext[0], up, un, ext[2])
    heat = heat_step(heat, up * sky, un * sky, ext[2] * sky)[:, 0:512]

    def level(r):
        edge = jnp.where(
            low40,
            pltpu.roll(haloB[1], lax.rem(128 - 2 * r, 128), 1),
            pltpu.roll(haloB[0], 126 - 2 * r, 1),
        )
        q = jnp.concatenate([qin[r], edge], axis=1)
        up, un, up2, un2 = (jnp.broadcast_to(coef[k, pl.ds(r, 1), :], (40, 640)) for k in range(4))
        q = tracer_step(tracer_step(q, up, un), up2, un2)
        qout[r] = q[:, 0:512]

    level(0)
    row8 = iota((8, 512), 0)
    rows_q = pltpu.roll(qout[0, 0:8, :], 2, 0)
    gath[x, 0:8, :] = heat[0:8]
    gath[x, 8:16, :] = jnp.where(row8 < 2, heat[8:16], jnp.where(row8 < 5, rows_q, 0.0))
    for k in range(3):
        send(gath.at[x], gath.at[x], sX.at[k], rX.at[k], lev=x_peers[k])
    for k in range(3):
        drain(gath.at[k], rX.at[k])
    product = dot(matrix, jnp.concatenate([gath[k] for k in range(4)], axis=0))
    top = product[32:33, :]

    @pl.when(jnp.logical_and(is_sky, half == 1))
    def _():
        piece[...] = jnp.where(
            x == 0, top[:, 0:128], jnp.where(x == 1, top[:, 128:256], jnp.where(x == 2, top[:, 256:384], top[:, 384:512]))
        )

        def body(k, _):
            send(piece, pieces.at[x, tile], sP, rP, comp=comp + 2, tile=k, lev=0)
            return 0

        lax.fori_loop(0, tiles, body, 0)

    @pl.when(jnp.logical_and(is_sky, half == 0))
    def _():
        line = jnp.where(
            x == 0, gath[0, 10:11, :], jnp.where(x == 1, gath[0, 11:12, :], jnp.where(x == 2, gath[0, 12:13, :], top))
        )
        for c in range(4):
            srow[c : c + 1, :] = line[:, c * 128 : (c + 1) * 128]

        def body(k, _):
            send(srow, rows.at[x, tile], sR, rR, comp=comp + 2, tile=lax.rem(tile + k, tiles), lev=0)
            return 0

        lax.fori_loop(0, tiles, body, 0)

    own[...] = product[0:16]
    for c in range(4):
        flip_s[pl.ds(c, 10, stride=4), :] = product[16:26, c * 128 : (c + 1) * 128]

    @pl.when(half == 1)
    def _():
        send(flip_s, flip_r, sF, rF, lev=other)

    def more(r, _):
        level(r)
        return 0

    lax.fori_loop(1, 10, more, 0)

    @pl.when(half == 0)
    def _():
        pl.semaphore_wait(ready, 1)
        send(flip_s, flip_r, sF, rF, lev=other)

    for c in loads[5:]:
        c.wait()

    @pl.when(is_wrap)
    def _():
        mine = ring.at[order, x]
        for g in range(1, 4):

            @pl.when(g > order)
            def _():
                drain(ring.at[g], rE.at[g])
                for k in range(4):
                    send(mine, mine, sE.at[g], rE.at[order], **group(g, k))

        drain(wrapB, rW)

        @pl.when(first)
        def _():
            send(sendB.at[1], wrapB, sW, rW, tile=tiles - 1)

        drain(ring.at[order, pl.ds(0, 3)], rE.at[order])
        for g in range(0, 3):

            @pl.when(g < order)
            def _():
                drain(ring.at[g], rE.at[g])

        up, un = courant(joined(ring[half * 2, x], ring[half * 2 + 1, x])[1])
        ring_coef[0] = up
        ring_coef[1] = un
        ring_coef[2] = up * sky
        ring_coef[3] = un * sky
        for flag, c, turn in ((first, 0, 126), (last, 3, 128)):

            @pl.when(flag)
            def _():
                def fix(r, _):
                    at = slice(c * 128, (c + 1) * 128)
                    far = pltpu.roll(wrapB[...], lax.rem(turn - 2 * r, 128), 1)
                    q = jnp.where(low40, qin[r, :, at], far) if c == 0 else jnp.where(low40, far, qin[r, :, at])
                    up, un, up2, un2 = (
                        jnp.broadcast_to(ring_coef[k, pl.ds(r, 1), :], (40, 128)) for k in range(4)
                    )
                    q = tracer_step(tracer_step(q, up, un), up2, un2)
                    new = lane40 < 2 if c == 0 else lane40 >= 126
                    qout[r, :, at] = jnp.where(new, q, qout[r, :, at])
                    return 0

                lax.fori_loop(0, 10, fix, 0)

    def edge_heat(from_right, from_left, again):
        t, u, d = joined(from_right, from_left)
        up, un = courant(u)
        return heat_step(heat_step(t, up, un, d), up * again, un * again, d * again)

    @pl.when(is_target)
    def _():
        drain(edge_r, rG)
        total = edge_heat(edge_r[0, 0], edge_r[1, 0], 1.0)
        for k in range(1, 8):
            total = total + edge_heat(edge_r[0, k], edge_r[1, k], 1.0)
        total = jnp.where(iota((16, 128), 0) < 10, total, 0.0)
        q, u, _ = joined(edge_r[0, 0], edge_r[1, 0])
        up, un = courant(jnp.broadcast_to(u[0:1], (8, 128)))
        edge_rows[...] = tracer_step(tracer_step(q[8:16], up, un), up, un)
        edge_rows[0:1, :] = jnp.sum(total, axis=0, keepdims=True)

    block = lax.shift_right_logical(i_s[0, 256], 9)
    before, after = lax.rem(block + tiles - 1, tiles), lax.rem(block + 1, tiles)
    lane1 = iota((1, 128), 1)

    def window(f):
        b, m, a = rows[f, before], rows[f, block], rows[f, after]
        w = [b[3:4]] + [m[c : c + 1] for c in range(4)] + [a[0:1]]
        if f == 3:
            extra = [pieces[3, before]] + [pieces[c, block] for c in range(4)] + [pieces[0, after]]
            w = [a + b for a, b in zip(w, extra)]
        edge = edge_rows[0:1, :] if f == 3 else edge_rows[2 + f : 3 + f, :]
        w[0] = jnp.where(lane1 >= jnp.where(before == tiles - 1, 126, 128), edge, w[0])
        w[1] = jnp.where(lane1 < jnp.where(block == 0, 2, 0), edge, w[1])
        w[4] = jnp.where(lane1 >= jnp.where(block == tiles - 1, 126, 128), edge, w[4])
        w[5] = jnp.where(lane1 < jnp.where(after == 0, 2, 0), edge, w[5])
        return w

    def remap(pair):
        windows = [window(f) for f in pair]
        for c in range(4):
            at = slice(c * 128, (c + 1) * 128)
            place = jnp.bitwise_and(i_v[:, at] - block * 512 + 128, tiles * 512 - 1)
            place = jnp.concatenate([place, place], axis=0)
            which, within = lax.shift_right_logical(place, 7), jnp.bitwise_and(place, 127)
            weight = w_v[:, at]
            sea = sea_v[c : c + 1, :] == 1
            got = jnp.zeros((8, 128), F32)
            for m in range(c, c + 3):
                source = jnp.concatenate([jnp.broadcast_to(w[m], (4, 128)) for w in windows], axis=0)
                taken = jnp.take_along_axis(source, within, axis=1, mode="promise_in_bounds")
                got = jnp.where(which == m, taken, got)
            for k, f in enumerate(pair):
                remapped = jnp.sum(got[4 * k : 4 * k + 4] * weight, axis=0, keepdims=True)
                if f < 3:
                    s = qout[0, f : f + 1, at]
                    qout[0, f : f + 1, at] = jnp.where(sea, s + 0.5 * (remapped - s), s)
                else:
                    s = tout[c : c + 1, :]
                    tout[c : c + 1, :] = jnp.where(sea, s + 0.5 * (remapped - s), s)

    @pl.when(is_target)
    def _():
        drain(rows, rR)
        remap((0, 1))

    drain(flip_r, rF)
    for c in range(4):
        tout[pl.ds(c, 10, stride=4), :] = own[0:10, c * 128 : (c + 1) * 128] + flip_r[pl.ds(c, 10, stride=4), :]

    @pl.when(is_wrap)
    def _():
        mixed_rows = dot(dot(pick_rows[0:16], m_v[...]), pick_cols(128, 0))
        stepped = [edge_heat(ring[2 * (k // 4), k % 4], ring[2 * (k // 4) + 1, k % 4], sky) for k in range(8)]
        mixed = dot(mixed_rows, jnp.concatenate(stepped, axis=0))[0:10]
        for flag, c, new in ((first, 0, lane < 2), (last, 3, lane >= 126)):

            @pl.when(flag)
            def _():
                tout[pl.ds(c, 10, stride=4), :] = jnp.where(new[0:10], mixed, tout[pl.ds(c, 10, stride=4), :])

    @pl.when(is_target)
    def _():
        drain(pieces, rP)
        remap((2, 3))

    @pl.when(tile < tiles - 1)
    def _():
        drain(sendA.at[0], sA.at[0])
        drain(sendB.at[0], sB.at[0])

    @pl.when(tile > 0)
    def _():
        drain(sendA.at[1], sA.at[1])
        drain(sendB.at[1], sB.at[1])

    for k in range(3):
        drain(gath.at[k], sX.at[k])
    drain(flip_s, sF)

    @pl.when(jnp.logical_and(is_sky, half == 0))
    def _():
        drain(rows.at[0], sR)

    @pl.when(jnp.logical_and(is_sky, half == 1))
    def _():
        drain(pieces.at[0], sP)

    @pl.when(is_wrap)
    def _():
        for g in range(4):

            @pl.when(g == order)
            def _():
                drain(ring.at[g, pl.ds(0, 3)], sE.at[g])

            @pl.when(g != order)
            def _():
                drain(ring.at[g], sE.at[g])

        drain(wrapB, sW)

        @pl.when(is_sky)
        def _():
            for k in range(2):
                drain(edge_r, sG)


def body(t, u, q, d, m, w, i, sea):
    hbm = pl.BlockSpec(memory_space=pltpu.HBM)
    vmem = pl.BlockSpec(memory_space=pltpu.VMEM)
    dma = pltpu.SemaphoreType.DMA
    tiles = lax.axis_size("tile")
    buf = lambda *s: pltpu.VMEM(s, F32)
    tout, qout = pl.pallas_call(
        kernel,
        out_shape=(jax.ShapeDtypeStruct((40, 128), F32), jax.ShapeDtypeStruct((10, 40, 512), F32)),
        in_specs=[hbm] * 8,
        out_specs=(vmem, vmem),
        scratch_shapes=[
            buf(40, 128), buf(40, 128), buf(40, 128), buf(10, 40, 512), buf(80, 80),
            buf(4, 512), pltpu.VMEM((4, 512), jnp.int32), pltpu.SMEM((4, 512), jnp.int32), pltpu.VMEM((4, 128), jnp.int32),
            buf(3, 16, 640), buf(4, 16, 640), buf(2, 16, 128), buf(2, 40, 128), buf(2, 16, 128), buf(2, 40, 128),
            buf(4, 16, 512), buf(40, 128), buf(40, 128), buf(16, 512), buf(4, 128), buf(1, 128),
            buf(4, tiles, 4, 128), buf(4, tiles, 1, 128),
            buf(4, 4, 16, 128), buf(4, 16, 128), buf(40, 128), buf(16, 128), buf(2, 8, 16, 128), buf(8, 128),
            dma((9,)), dma((2,)), dma((2,)), dma((2,)), dma((2,)), dma((3,)), dma((3,)), dma, dma,
            dma, dma, dma, dma, dma((4,)), dma((4,)), dma, dma, dma, dma, pltpu.SemaphoreType.REGULAR,
        ],
        compiler_params=pltpu.CompilerParams(
            collective_id=0, has_side_effects=True, vmem_limit_bytes=24 * 1024 * 1024
        ),
    )(
        t.reshape(40, 128), u.reshape(40, 128), d.reshape(40, 128), jnp.transpose(q[0], (1, 0, 2)),
        m[0], w.T, i.T, sea.reshape(4, 128),
    )
    return tout.reshape(1, 10, 512), jnp.transpose(qout, (1, 0, 2))[None]


def solution(mesh):
    in_specs = (
        P("comp", "lev", "tile"),
        P("comp", "lev", "tile"),
        P("comp", None, "lev", "tile"),
        P("comp", "lev", "tile"),
        P("comp", None, None),
        P("tile", None),
        P("tile", None),
        P("tile"),
    )
    out_specs = (P("comp", "lev", "tile"), P("comp", None, "lev", "tile"))
    return jax.shard_map(body, mesh=mesh, in_specs=in_specs, out_specs=out_specs, check_vma=False)
```

time: 67 us -> 54.1 us (0.81)
  Pallas kernels: 58.8 us -> 45.5 us
    pallas_call x1, Pallas kernels: 58.8 us -> 45.5 us  [body(): pl.pallas_call(kernel, out_shape=(jax.ShapeDtypeStruct((40, 128), F32), j...]
where the time goes in v2:
time: 54.1 us; the launch traced here: 53.2 us
  Pallas kernels  45.5 us (84%)
  local copies, waits for them, and re-layouts  6.98 us (13%)
  between operations  0.66 us (1%)
    pallas_call x1, Pallas kernels, body(): pl.pallas_call(kernel, out_shape=(jax.ShapeDtypeStruct((40, 128), F32), j...  45.5 us
    unnamed x18, local copies, waits for them, and re-layouts  6.98 us

profile of v2, /device:TPU:24, one launch (start us, length us, event | category | flops | bytes accessed | tf_op | source)
XLA Modules:
  0.0 53.2 jit_solution(12453540642009320716)
XLA Ops:
  0.6 0.0 copy-start.5
  0.6 0.0 copy-start.7
  0.7 0.7 %copy-done.5 = f32[512,4]{0,1:T(4,128)S(1)} copy-done((f32[512,4]{0,1:T(4,128)S(1)}, f32[512,4]{0,1:T(4,128)}, u32[]{:S(2)}) %copy-start.5) | copy-done | bytes 8216
  1.3 0.0 copy-done.7
  1.3 0.0 copy-start
  1.3 1.1 %copy-done = f32[1,40,10,512]{3,1,2,0:T(8,128)S(1)} copy-done((f32[1,40,10,512]{3,1,2,0:T(8,128)S(1)}, f32[1,40,10,512]{3,1,2,0:T(8,128)}, u32[]{:S(2)}) %copy-start) | copy-done | bytes 819224
  2.5 0.0 copy-start.1
  2.5 0.8 %copy-done.1 = f32[1,80,80]{2,1,0:T(8,128)S(1)} copy-done((f32[1,80,80]{2,1,0:T(8,128)S(1)}, f32[1,80,80]{2,1,0:T(8,128)}, u32[]{:S(2)}) %copy-start.1) | copy-done | bytes 25624
  3.3 0.0 copy-start.2
  3.3 0.7 %copy-done.2 = f32[1,10,512]{2,0,1:T(1,128)S(1)} copy-done((f32[1,10,512]{2,0,1:T(1,128)S(1)}, f32[1,10,512]{2,0,1:T(1,128)}, u32[]{:S(2)}) %copy-start.2) | copy-done | bytes 20504
  4.0 0.0 copy-start.3
  4.0 0.7 %copy-done.3 = f32[1,10,512]{2,0,1:T(1,128)S(1)} copy-done((f32[1,10,512]{2,0,1:T(1,128)S(1)}, f32[1,10,512]{2,0,1:T(1,128)}, u32[]{:S(2)}) %copy-start.3) | copy-done | bytes 20504
  4.7 0.0 copy-start.4
  4.7 0.7 %copy-done.4 = f32[1,10,512]{2,0,1:T(1,128)S(1)} copy-done((f32[1,10,512]{2,0,1:T(1,128)S(1)}, f32[1,10,512]{2,0,1:T(1,128)}, u32[]{:S(2)}) %copy-start.4) | copy-done | bytes 20504
  5.4 0.0 copy-start.6
  5.4 0.7 %copy-done.6 = s32[512,4]{0,1:T(4,128)S(1)} copy-done((s32[512,4]{0,1:T(4,128)S(1)}, s32[512,4]{0,1:T(4,128)}, u32[]{:S(2)}) %copy-start.6) | copy-done | bytes 8216
  6.1 45.5 %shard_map.95 = (f32[40,128]{1,0:T(8,128)S(1)}, f32[10,40,512]{2,1,0:T(8,128)S(1)}) custom-call(f32[40,128]{1,0:T(8,128)S(1)} %bitcast.18, f32[40,128]{1,0:T(8,128)S(1)} %bitcast.19, f32[40,128]{1,0:T(8,128)S(1)} %bitcast.20, f32[10,40,512]{2,1,0:T(8,128)S(1)} %bitcast.14, f32[80,80]{1,0:T(8,128)S(1)} %bitcast.16, f32[4,512]{1,0:T(4,128)S(1)} %bitcast.21, ...), custom_call_target="tpu_custom_call" | custom-call | tf_op jit(solution)/shard_map/pallas_call | solution.py:515
  51.7 0.6 %copy.14 = f32[1,10,512]{2,0,1:T(1,128)} copy(f32[1,10,512]{2,0,1:T(1,128)S(1)} %bitcast.17) | data formatting | bytes 40960
  52.3 0.9 %copy.15 = f32[1,40,10,512]{3,1,2,0:T(8,128)} copy(f32[1,40,10,512]{3,1,2,0:T(8,128)S(1)} %bitcast.15) | data formatting | bytes 1638400
Async XLA Ops:
  0.6 0.7 %copy-start.5 = (f32[512,4]{0,1:T(4,128)S(1)}, f32[512,4]{0,1:T(4,128)}, u32[]{:S(2)}) copy-start(f32[512,4]{0,1:T(4,128)} %param.13) | copy-start | bytes 24580
  0.6 0.7 %copy-start.7 = (s32[512]{0:T(512)S(1)}, s32[512]{0:T(512)}, u32[]{:S(2)}) copy-start(s32[512]{0:T(512)} %param.15) | copy-start | bytes 6148
  1.3 1.1 %copy-start = (f32[1,40,10,512]{3,1,2,0:T(8,128)S(1)}, f32[1,40,10,512]{3,1,2,0:T(8,128)}, u32[]{:S(2)}) copy-start(f32[1,40,10,512]{3,1,2,0:T(8,128)} %param.10) | copy-start | bytes 2457604
  2.5 0.8 %copy-start.1 = (f32[1,80,80]{2,1,0:T(8,128)S(1)}, f32[1,80,80]{2,1,0:T(8,128)}, u32[]{:S(2)}) copy-start(f32[1,80,80]{2,1,0:T(8,128)} %param.12) | copy-start | bytes 76804
  3.3 0.7 %copy-start.2 = (f32[1,10,512]{2,0,1:T(1,128)S(1)}, f32[1,10,512]{2,0,1:T(1,128)}, u32[]{:S(2)}) copy-start(f32[1,10,512]{2,0,1:T(1,128)} %param.8) | copy-start | bytes 61444
  4.0 0.7 %copy-start.3 = (f32[1,10,512]{2,0,1:T(1,128)S(1)}, f32[1,10,512]{2,0,1:T(1,128)}, u32[]{:S(2)}) copy-start(f32[1,10,512]{2,0,1:T(1,128)} %param.9) | copy-start | bytes 61444
  4.7 0.7 %copy-start.4 = (f32[1,10,512]{2,0,1:T(1,128)S(1)}, f32[1,10,512]{2,0,1:T(1,128)}, u32[]{:S(2)}) copy-start(f32[1,10,512]{2,0,1:T(1,128)} %param.11) | copy-start | bytes 61444
  5.4 0.7 %copy-start.6 = (s32[512,4]{0,1:T(4,128)S(1)}, s32[512,4]{0,1:T(4,128)}, u32[]{:S(2)}) copy-start(s32[512,4]{0,1:T(4,128)} %param.14) | copy-start | bytes 24580

commit v3 on v2

--- a/solution.py
+++ b/solution.py
@@ -66,7 +66,7 @@
     tout, qout,
     t40, u40, d40, qin, m_v, w_v, i_v, i_s, sea_v,
     ext, coef, sendA, sendB, haloA, haloB, gath, flip_s, flip_r, own, srow, piece, rows, pieces,
-    ring, ring_coef, wrapB, edge_s, edge_r, edge_rows,
+    ring, ring_coef, wrapB, edge_s, edge_rows, mixed_rows, mixed_v,
     in_sem, sA, rA, sB, rB, sX, rX, sF, rF, sR, rR, sP, rP, sE, rE, sW, rW, sG, rG, ready,
 ):
     comp, tile, lev = lax.axis_index("comp"), lax.axis_index("tile"), lax.axis_index("lev")
@@ -123,7 +123,7 @@
     @pl.when(is_target)
     def _():
         def body(k, _):
-            for j in range(8):
+            for j in (0, 4):
                 hello(comp=comp - 2, tile=lax.rem(tile + k, tiles), lev=j)
             return 0
 
@@ -175,7 +175,7 @@
 
     greeted = (
         jnp.where(tile > 0, 1, 0) + jnp.where(tile < tiles - 1, 1, 0) + 3 + half
-        + jnp.where(is_sky, tiles, 0) + jnp.where(is_wrap, 4 * order, 0)
+        + jnp.where(jnp.logical_and(is_sky, x == 0), tiles, 0) + jnp.where(is_wrap, 4 * order, 0)
     )
     pl.semaphore_wait(bar, greeted)
 
@@ -206,7 +206,10 @@
 
     @pl.when(is_wrap)
     def _():
-        ring[order, x] = jnp.where(last, sendA[0], sendA[1])
+        edge = jnp.where(last, sendA[0], sendA[1])
+        q3 = pltpu.roll(jnp.where(last, qin[0, 0:8, 384:512], qin[0, 0:8, 0:128]), 2, 0)
+        ring[order, x, 0:8] = edge[0:8]
+        ring[order, x, 8:16] = jnp.where(iota((8, 128), 0) < 2, edge[8:16], q3)
         mine = ring.at[order, x]
         for p in x_peers:
             send(mine, mine, sE.at[order], rE.at[order], lev=p)
@@ -221,27 +224,13 @@
         def _():
             send(sendB.at[0], wrapB, sW, rW, tile=0)
 
-        @pl.when(is_sky)
-        def _():
-            i, j = iota((16, 80), 0), iota((16, 80), 1)
-            here = jnp.logical_and(i < 10, j == lev * 10 + i)
-            scale = jnp.sum(jnp.where(here, jnp.broadcast_to(m_v[0:1, :], (16, 80)), 0.0), axis=1, keepdims=True)
-            is_t = jnp.where(last, lane - 124, 3 - lane) >= 0
-            edge = ring[order, x]
-            edge = jnp.where(is_t, edge * scale, edge)
-            q3 = jnp.where(last, qin[0, 0:8, 384:512], qin[0, 0:8, 0:128])
-            low8 = iota((8, 128), 0) < 2
-            edge_s[0:8] = edge[0:8]
-            edge_s[8:16] = jnp.where(low8, edge[8:16], pltpu.roll(q3, 2, 0))
-            side = jnp.where(last, 1, 0)
-
-            def body(k, _):
-                send(edge_s, edge_r.at[side, lev], sG, rG, comp=comp + 2, tile=lax.rem(tile + k, tiles), lev=0)
-                return 0
-
-            lax.fori_loop(0, tiles, body, 0)
-
-    matrix = dot(dot(pick_rows, m_v[...]), pick_cols(64, half * 40))
+    picked = dot(pick_rows, m_v[...])
+    matrix = dot(picked, pick_cols(64, half * 40))
+
+    @pl.when(is_wrap)
+    def _():
+        mixed_rows[...] = dot(picked[0:16], pick_cols(128, 0))
+
 
     @pl.when(tile > 0)
     def _():
@@ -321,6 +310,45 @@
     def _():
         send(flip_s, flip_r, sF, rF, lev=other)
 
+    def edge_heat(from_right, from_left, again):
+        t, u, d = joined(from_right, from_left)
+        up, un = courant(u)
+        return heat_step(heat_step(t, up, un, d), up * again, un * again, d * again)
+
+    def answer_later_ones(mine_order):
+        mine = ring.at[mine_order, x]
+        for g in range(mine_order + 1, 4):
+            drain(ring.at[g], rE.at[g])
+            for k in range(4):
+                send(mine, mine, sE.at[g], rE.at[mine_order], **group(g, k))
+            if mine_order % 2 == 0 and g == mine_order + 1:
+                send(sendB.at[1], wrapB, sW, rW, tile=tiles - 1)
+
+    def mix_edges(mine_order):
+        drain(ring.at[mine_order, pl.ds(0, 3)], rE.at[mine_order])
+        for g in range(mine_order):
+            drain(ring.at[g], rE.at[g])
+        stepped = [edge_heat(ring[2 * (k // 4), k % 4], ring[2 * (k // 4) + 1, k % 4], sky) for k in range(8)]
+        mixed_v[...] = dot(mixed_rows[...], jnp.concatenate(stepped, axis=0))
+
+    @pl.when(jnp.logical_and(first, half == 0))
+    def _():
+        answer_later_ones(0)
+        mix_edges(0)
+
+        @pl.when(jnp.logical_and(is_sky, lev == 0))
+        def _():
+            q, u, _ = joined(ring[0, 0], ring[1, 0])
+            up, un = courant(jnp.broadcast_to(u[0:1], (8, 128)))
+            edge_s[...] = tracer_step(tracer_step(q[8:16], up, un), up, un)
+            edge_s[0:1, :] = mixed_v[0:1, :]
+
+            def body(k, _):
+                send(edge_s, edge_rows, sG, rG, comp=comp + 2, tile=k, lev=0)
+                return 0
+
+            lax.fori_loop(0, tiles, body, 0)
+
     def more(r, _):
         level(r)
         return 0
@@ -335,30 +363,16 @@
     for c in loads[5:]:
         c.wait()
 
+    for g in range(1, 4):
+
+        @pl.when(jnp.logical_and(is_wrap, order == g))
+        def _():
+            answer_later_ones(g)
+            mix_edges(g)
+
     @pl.when(is_wrap)
     def _():
-        mine = ring.at[order, x]
-        for g in range(1, 4):
-
-            @pl.when(g > order)
-            def _():
-                drain(ring.at[g], rE.at[g])
-                for k in range(4):
-                    send(mine, mine, sE.at[g], rE.at[order], **group(g, k))
-
         drain(wrapB, rW)
-
-        @pl.when(first)
-        def _():
-            send(sendB.at[1], wrapB, sW, rW, tile=tiles - 1)
-
-        drain(ring.at[order, pl.ds(0, 3)], rE.at[order])
-        for g in range(0, 3):
-
-            @pl.when(g < order)
-            def _():
-                drain(ring.at[g], rE.at[g])
-
         up, un = courant(joined(ring[half * 2, x], ring[half * 2 + 1, x])[1])
         ring_coef[0] = up
         ring_coef[1] = un
@@ -381,23 +395,6 @@
                     return 0
 
                 lax.fori_loop(0, 10, fix, 0)
-
-    def edge_heat(from_right, from_left, again):
-        t, u, d = joined(from_right, from_left)
-        up, un = courant(u)
-        return heat_step(heat_step(t, up, un, d), up * again, un * again, d * again)
-
-    @pl.when(is_target)
-    def _():
-        drain(edge_r, rG)
-        total = edge_heat(edge_r[0, 0], edge_r[1, 0], 1.0)
-        for k in range(1, 8):
-            total = total + edge_heat(edge_r[0, k], edge_r[1, k], 1.0)
-        total = jnp.where(iota((16, 128), 0) < 10, total, 0.0)
-        q, u, _ = joined(edge_r[0, 0], edge_r[1, 0])
-        up, un = courant(jnp.broadcast_to(u[0:1], (8, 128)))
-        edge_rows[...] = tracer_step(tracer_step(q[8:16], up, un), up, un)
-        edge_rows[0:1, :] = jnp.sum(total, axis=0, keepdims=True)
 
     block = lax.shift_right_logical(i_s[0, 256], 9)
     before, after = lax.rem(block + tiles - 1, tiles), lax.rem(block + 1, tiles)
@@ -441,6 +438,7 @@
 
     @pl.when(is_target)
     def _():
+        drain(edge_rows, rG)
         drain(rows, rR)
         remap((0, 1))
 
@@ -450,9 +448,7 @@
 
     @pl.when(is_wrap)
     def _():
-        mixed_rows = dot(dot(pick_rows[0:16], m_v[...]), pick_cols(128, 0))
-        stepped = [edge_heat(ring[2 * (k // 4), k % 4], ring[2 * (k // 4) + 1, k % 4], sky) for k in range(8)]
-        mixed = dot(mixed_rows, jnp.concatenate(stepped, axis=0))[0:10]
+        mixed = mixed_v[0:10, :]
         for flag, c, new in ((first, 0, lane < 2), (last, 3, lane >= 126)):
 
             @pl.when(flag)
@@ -500,10 +496,10 @@
 
         drain(wrapB, sW)
 
-        @pl.when(is_sky)
+        @pl.when(jnp.logical_and(is_sky, jnp.logical_and(first, lev == 0)))
         def _():
-            for k in range(2):
-                drain(edge_r, sG)
+            drain(rows.at[0], sG)
+            drain(rows.at[0], sG)
 
 
 def body(t, u, q, d, m, w, i, sea):
@@ -523,7 +519,7 @@
             buf(3, 16, 640), buf(4, 16, 640), buf(2, 16, 128), buf(2, 40, 128), buf(2, 16, 128), buf(2, 40, 128),
             buf(4, 16, 512), buf(40, 128), buf(40, 128), buf(16, 512), buf(4, 128), buf(1, 128),
             buf(4, tiles, 4, 128), buf(4, tiles, 1, 128),
-            buf(4, 4, 16, 128), buf(4, 16, 128), buf(40, 128), buf(16, 128), buf(2, 8, 16, 128), buf(8, 128),
+            buf(4, 4, 16, 128), buf(4, 16, 128), buf(40, 128), buf(8, 128), buf(8, 128), buf(16, 128), buf(16, 128),
             dma((9,)), dma((2,)), dma((2,)), dma((2,)), dma((2,)), dma((3,)), dma((3,)), dma, dma,
             dma, dma, dma, dma, dma((4,)), dma((4,)), dma, dma, dma, dma, pltpu.SemaphoreType.REGULAR,
         ],
@@ -531,8 +527,13 @@
             collective_id=0, has_side_effects=True, vmem_limit_bytes=24 * 1024 * 1024
         ),
     )(
-        t.reshape(40, 128), u.reshape(40, 128), d.reshape(40, 128), jnp.transpose(q[0], (1, 0, 2)),
-        m[0], w.T, i.T, sea.reshape(4, 128),
+        *(
+            pltpu.with_memory_space_constraint(v, pltpu.HBM)
+            for v in (
+                t.reshape(40, 128), u.reshape(40, 128), d.reshape(40, 128), jnp.transpose(q[0], (1, 0, 2)),
+                m[0], w.T, i.T, sea.reshape(4, 128),
+            )
+        )
     )
     return tout.reshape(1, 10, 512), jnp.transpose(qout, (1, 0, 2))[None]
 

time: 54.1 us -> 47.5 us (0.88)
  local copies, waits for them, and re-layouts: 6.98 us -> 1.5 us
  Pallas kernels: 45.5 us -> 44.7 us
    unnamed x18 -> x2, local copies, waits for them, and re-layouts: 6.98 us -> 1.5 us
    pallas_call x1, Pallas kernels: 45.5 us -> 44.7 us  [body(): pl.pallas_call(kernel, out_shape=(jax.ShapeDtypeStruct((40, 128), F32), j...]
where the time goes in v3:
time: 47.5 us; the launch traced here: 46.8 us
  Pallas kernels  44.7 us (94%)
  local copies, waits for them, and re-layouts  1.5 us (3%)
  between operations  0.64 us (1%)
    pallas_call x1, Pallas kernels, body(): pl.pallas_call(kernel, out_shape=(jax.ShapeDtypeStruct((40, 128), F32), j...  44.7 us
    unnamed x2, local copies, waits for them, and re-layouts  1.5 us

profile of v3, /device:TPU:24, one launch (start us, length us, event | category | flops | bytes accessed | tf_op | source)
XLA Modules:
  0.0 46.8 jit_solution(18077809893075899887)
XLA Ops:
  0.6 44.7 %shard_map.95 = (f32[40,128]{1,0:T(8,128)S(1)}, f32[10,40,512]{2,1,0:T(8,128)S(1)}) custom-call(f32[40,128]{1,0:T(8,128)} %bitcast.18, f32[40,128]{1,0:T(8,128)} %bitcast.19, f32[40,128]{1,0:T(8,128)} %bitcast.20, f32[10,40,512]{2,1,0:T(8,128)} %bitcast.16, f32[80,80]{1,0:T(8,128)} %bitcast.17, f32[4,512]{1,0:T(4,128)} %bitcast.21, s32[4,512]{1,0:T(4,128)} %bitcast.22, ...), custom_call_target="tpu_custom_call" | custom-call | tf_op jit(solution)/shard_map/pallas_call | solution.py:511
  45.3 0.6 %copy.14 = f32[1,10,512]{2,0,1:T(1,128)} copy(f32[1,10,512]{2,0,1:T(1,128)S(1)} %bitcast.15) | data formatting | bytes 40960
  45.9 0.9 %copy.15 = f32[1,40,10,512]{3,1,2,0:T(8,128)} copy(f32[1,40,10,512]{3,1,2,0:T(8,128)S(1)} %bitcast.14) | data formatting | bytes 1638400

commit v4 on v3

--- a/solution.py
+++ b/solution.py
@@ -66,8 +66,8 @@
     tout, qout,
     t40, u40, d40, qin, m_v, w_v, i_v, i_s, sea_v,
     ext, coef, sendA, sendB, haloA, haloB, gath, flip_s, flip_r, own, srow, piece, rows, pieces,
-    ring, ring_coef, wrapB, edge_s, edge_rows, mixed_rows, mixed_v,
-    in_sem, sA, rA, sB, rB, sX, rX, sF, rF, sR, rR, sP, rP, sE, rE, sW, rW, sG, rG, ready,
+    ring, ring_coef, wrapB, edge_s, edge_rows, mixed_rows, mixed_v, relayB, answer, reply,
+    in_sem, sA, rA, sB, rB, sX, rX, sF, rF, sR, rR, sP, rP, sE, rE, sW, rW, sG, rG, sV, rV, ready, go,
 ):
     comp, tile, lev = lax.axis_index("comp"), lax.axis_index("tile"), lax.axis_index("lev")
     tiles = lax.axis_size("tile")
@@ -77,6 +77,9 @@
     first, last = tile == 0, tile == tiles - 1
     is_wrap = jnp.logical_or(first, last)
     order = half * 2 + jnp.where(last, 1, 0)
+    is_teller = jnp.logical_and(comp >= 2, x == 1)
+    is_early = jnp.logical_and(half == 0, tile < tiles // 2)
+    is_hub = jnp.logical_and(first, half == 0)
     x_peers = [half * 4 + lax.rem(x + k, 4) for k in range(1, 4)]
     other = lax.rem(lev + 4, 8)
 
@@ -111,20 +114,25 @@
     def _():
         hello(lev=lev + 4)
 
-    @pl.when(is_wrap)
+    @pl.when(is_sky)
+    def _():
+        hello(comp=comp + 2, lev=half * 4 + 1)
+
+    @pl.when(is_hub)
     def _():
         for g in range(1, 4):
-
-            @pl.when(g > order)
-            def _():
-                for k in range(4):
-                    hello(**group(g, k))
+            for k in range(4):
+                hello(**group(g, k))
 
     @pl.when(is_target)
     def _():
         def body(k, _):
-            for j in (0, 4):
-                hello(comp=comp - 2, tile=lax.rem(tile + k, tiles), lev=j)
+            for j in (1, 5):
+
+                @pl.when(jnp.logical_or(k > 0, j > 1))
+                def _():
+                    hello(tile=lax.rem(tile + k, tiles), lev=j)
+
             return 0
 
         lax.fori_loop(0, tiles, body, 0)
@@ -175,7 +183,7 @@
 
     greeted = (
         jnp.where(tile > 0, 1, 0) + jnp.where(tile < tiles - 1, 1, 0) + 3 + half
-        + jnp.where(jnp.logical_and(is_sky, x == 0), tiles, 0) + jnp.where(is_wrap, 4 * order, 0)
+        + jnp.where(is_teller, tiles + 4 - jnp.where(half == 0, 1, 0), 0) + jnp.where(jnp.logical_and(is_wrap, order > 0), 4, 0)
     )
     pl.semaphore_wait(bar, greeted)
 
@@ -192,6 +200,12 @@
     @pl.when(half == 1)
     def _():
         pl.semaphore_signal(ready, inc=1, device_id={"lev": lev - 4}, device_id_type=MESH)
+
+    @pl.when(is_teller)
+    def _():
+        for k in range(4):
+            where = {"comp": comp - 2, "lev": half * 4 + k}
+            pl.semaphore_signal(go, inc=1, device_id=where, device_id_type=MESH)
 
     loads[4].wait()
     i, j = iota((48, 80), 0), iota((48, 80), 1)
@@ -211,25 +225,35 @@
         ring[order, x, 0:8] = edge[0:8]
         ring[order, x, 8:16] = jnp.where(iota((8, 128), 0) < 2, edge[8:16], q3)
         mine = ring.at[order, x]
-        for p in x_peers:
-            send(mine, mine, sE.at[order], rE.at[order], lev=p)
-        for g in range(0, 3):
-
-            @pl.when(g < order)
-            def _():
-                for k in range(4):
-                    send(mine, mine, sE.at[g], rE.at[order], **group(g, k))
-
-        @pl.when(last)
+
+        @pl.when(order == 0)
+        def _():
+            for p in x_peers:
+                send(mine, mine, sE.at[0], rE.at[0], lev=p)
+
+        @pl.when(order > 0)
+        def _():
+            for k in range(4):
+                send(mine, mine, sE.at[0], rE.at[order], **group(0, k))
+
+        @pl.when(order == 1)
         def _():
             send(sendB.at[0], wrapB, sW, rW, tile=0)
+
+        @pl.when(order == 2)
+        def _():
+            send(sendB.at[1], relayB.at[0], sW, rV.at[0], tile=0, lev=x)
+
+        @pl.when(order == 3)
+        def _():
+            send(sendB.at[0], relayB.at[1], sW, rV.at[1], tile=0, lev=x)
 
     picked = dot(pick_rows, m_v[...])
     matrix = dot(picked, pick_cols(64, half * 40))
 
     @pl.when(is_wrap)
     def _():
-        mixed_rows[...] = dot(picked[0:16], pick_cols(128, 0))
+        mixed_rows[...] = dot(picked[0:32], pick_cols(128, 0))
 
 
     @pl.when(tile > 0)
@@ -263,6 +287,13 @@
         up, un, up2, un2 = (jnp.broadcast_to(coef[k, pl.ds(r, 1), :], (40, 640)) for k in range(4))
         q = tracer_step(tracer_step(q, up, un), up2, un2)
         qout[r] = q[:, 0:512]
+
+    def tracers_inside():
+        def more(r, _):
+            level(r)
+            return 0
+
+        lax.fori_loop(1, 10, more, 0)
 
     level(0)
     row8 = iota((8, 512), 0)
@@ -276,6 +307,14 @@
     product = dot(matrix, jnp.concatenate([gath[k] for k in range(4)], axis=0))
     top = product[32:33, :]
 
+    @pl.when(is_early)
+    def _():
+        tracers_inside()
+
+    @pl.when(is_sky)
+    def _():
+        pl.semaphore_wait(go, 1)
+
     @pl.when(jnp.logical_and(is_sky, half == 1))
     def _():
         piece[...] = jnp.where(
@@ -315,26 +354,14 @@
         up, un = courant(u)
         return heat_step(heat_step(t, up, un, d), up * again, un * again, d * again)
 
-    def answer_later_ones(mine_order):
-        mine = ring.at[mine_order, x]
-        for g in range(mine_order + 1, 4):
-            drain(ring.at[g], rE.at[g])
-            for k in range(4):
-                send(mine, mine, sE.at[g], rE.at[mine_order], **group(g, k))
-            if mine_order % 2 == 0 and g == mine_order + 1:
-                send(sendB.at[1], wrapB, sW, rW, tile=tiles - 1)
-
-    def mix_edges(mine_order):
-        drain(ring.at[mine_order, pl.ds(0, 3)], rE.at[mine_order])
-        for g in range(mine_order):
+    @pl.when(is_hub)
+    def _():
+        drain(ring.at[0, pl.ds(0, 3)], rE.at[0])
+        for g in range(1, 4):
             drain(ring.at[g], rE.at[g])
         stepped = [edge_heat(ring[2 * (k // 4), k % 4], ring[2 * (k // 4) + 1, k % 4], sky) for k in range(8)]
-        mixed_v[...] = dot(mixed_rows[...], jnp.concatenate(stepped, axis=0))
-
-    @pl.when(jnp.logical_and(first, half == 0))
-    def _():
-        answer_later_ones(0)
-        mix_edges(0)
+        mixed = dot(mixed_rows[...], jnp.concatenate(stepped, axis=0))
+        mixed_v[...] = mixed[0:16]
 
         @pl.when(jnp.logical_and(is_sky, lev == 0))
         def _():
@@ -349,11 +376,22 @@
 
             lax.fori_loop(0, tiles, body, 0)
 
-    def more(r, _):
-        level(r)
-        return 0
-
-    lax.fori_loop(1, 10, more, 0)
+        answer[0, 0] = mixed[0:16]
+        answer[1, 0] = mixed[16:32]
+        answer[2, 0] = mixed[16:32]
+        answer[0, 1] = ring[0, x]
+        answer[1, 1] = ring[3, x]
+        answer[2, 1] = ring[2, x]
+        for g in range(1, 4):
+            send(answer.at[g - 1], reply, sE.at[g], rE.at[0], **group(g, x))
+        for k in range(2):
+            drain(relayB.at[k], rV.at[k])
+        for g, edge in ((1, sendB.at[1]), (2, relayB.at[1]), (3, relayB.at[0])):
+            send(edge, wrapB, sV.at[g - 1], rW, **group(g, x))
+
+    @pl.when(jnp.logical_not(is_early))
+    def _():
+        tracers_inside()
 
     @pl.when(half == 0)
     def _():
@@ -363,12 +401,11 @@
     for c in loads[5:]:
         c.wait()
 
-    for g in range(1, 4):
-
-        @pl.when(jnp.logical_and(is_wrap, order == g))
-        def _():
-            answer_later_ones(g)
-            mix_edges(g)
+    @pl.when(jnp.logical_and(is_wrap, order > 0))
+    def _():
+        drain(reply, rE.at[0])
+        mixed_v[...] = reply[0]
+        ring[half * 2 + jnp.where(last, 0, 1), x] = reply[1]
 
     @pl.when(is_wrap)
     def _():
@@ -484,17 +521,17 @@
 
     @pl.when(is_wrap)
     def _():
-        for g in range(4):
-
-            @pl.when(g == order)
-            def _():
-                drain(ring.at[g, pl.ds(0, 3)], sE.at[g])
-
-            @pl.when(g != order)
-            def _():
-                drain(ring.at[g], sE.at[g])
-
-        drain(wrapB, sW)
+        @pl.when(order > 0)
+        def _():
+            drain(ring.at[0], sE.at[0])
+            drain(wrapB, sW)
+
+        @pl.when(order == 0)
+        def _():
+            drain(ring.at[0, pl.ds(0, 3)], sE.at[0])
+            for g in range(1, 4):
+                drain(reply, sE.at[g])
+                drain(wrapB, sV.at[g - 1])
 
         @pl.when(jnp.logical_and(is_sky, jnp.logical_and(first, lev == 0)))
         def _():
@@ -519,9 +556,10 @@
             buf(3, 16, 640), buf(4, 16, 640), buf(2, 16, 128), buf(2, 40, 128), buf(2, 16, 128), buf(2, 40, 128),
             buf(4, 16, 512), buf(40, 128), buf(40, 128), buf(16, 512), buf(4, 128), buf(1, 128),
             buf(4, tiles, 4, 128), buf(4, tiles, 1, 128),
-            buf(4, 4, 16, 128), buf(4, 16, 128), buf(40, 128), buf(8, 128), buf(8, 128), buf(16, 128), buf(16, 128),
+            buf(4, 4, 16, 128), buf(4, 16, 128), buf(40, 128), buf(8, 128), buf(8, 128), buf(32, 128), buf(16, 128),
+            buf(2, 40, 128), buf(3, 2, 16, 128), buf(2, 16, 128),
             dma((9,)), dma((2,)), dma((2,)), dma((2,)), dma((2,)), dma((3,)), dma((3,)), dma, dma,
-            dma, dma, dma, dma, dma((4,)), dma((4,)), dma, dma, dma, dma, pltpu.SemaphoreType.REGULAR,
+            dma, dma, dma, dma, dma((4,)), dma((4,)), dma, dma, dma, dma, dma((3,)), dma((2,)), pltpu.SemaphoreType.REGULAR, pltpu.SemaphoreType.REGULAR,
         ],
         compiler_params=pltpu.CompilerParams(
             collective_id=0, has_side_effects=True, vmem_limit_bytes=24 * 1024 * 1024

time: 47.5 us -> 46 us (0.968)
  the two profiles are of different devices: /device:TPU:24 before, /device:TPU:1 now
where the time goes in v4:
time: 46 us; the launch traced here: 45.8 us
  Pallas kernels  43.7 us (95%)
  local copies, waits for them, and re-layouts  1.5 us (3%)
  between operations  0.64 us (1%)
    pallas_call x1, Pallas kernels, body(): pl.pallas_call(kernel, out_shape=(jax.ShapeDtypeStruct((40, 128), F32), j...  43.7 us
    unnamed x2, local copies, waits for them, and re-layouts  1.5 us

profile of v4, /device:TPU:1, one launch (start us, length us, event | category | flops | bytes accessed | tf_op | source)
XLA Modules:
  0.0 45.8 jit_solution(11520260410523209700)
XLA Ops:
  0.6 43.7 %shard_map.95 = (f32[40,128]{1,0:T(8,128)S(1)}, f32[10,40,512]{2,1,0:T(8,128)S(1)}) custom-call(f32[40,128]{1,0:T(8,128)} %bitcast.18, f32[40,128]{1,0:T(8,128)} %bitcast.19, f32[40,128]{1,0:T(8,128)} %bitcast.20, f32[10,40,512]{2,1,0:T(8,128)} %bitcast.16, f32[80,80]{1,0:T(8,128)} %bitcast.17, f32[4,512]{1,0:T(4,128)} %bitcast.21, s32[4,512]{1,0:T(4,128)} %bitcast.22, ...), custom_call_target="tpu_custom_call" | custom-call | tf_op jit(solution)/shard_map/pallas_call | solution.py:548
  44.3 0.6 %copy.14 = f32[1,10,512]{2,0,1:T(1,128)} copy(f32[1,10,512]{2,0,1:T(1,128)S(1)} %bitcast.15) | data formatting | bytes 40960
  44.9 0.9 %copy.15 = f32[1,40,10,512]{3,1,2,0:T(8,128)} copy(f32[1,40,10,512]{3,1,2,0:T(8,128)S(1)} %bitcast.14) | data formatting | bytes 1638400

commit v5 on v4

--- a/solution.py
+++ b/solution.py
@@ -66,8 +66,8 @@
     tout, qout,
     t40, u40, d40, qin, m_v, w_v, i_v, i_s, sea_v,
     ext, coef, sendA, sendB, haloA, haloB, gath, flip_s, flip_r, own, srow, piece, rows, pieces,
-    ring, ring_coef, wrapB, edge_s, edge_rows, mixed_rows, mixed_v, relayB, answer, reply,
-    in_sem, sA, rA, sB, rB, sX, rX, sF, rF, sR, rR, sP, rP, sE, rE, sW, rW, sG, rG, sV, rV, ready, go,
+    ring, ring_coef, wrapB, edge_s, edge_rows, mixed_rows, mixed_v, relayB, answer, reply, parts, landed,
+    in_sem, sA, rA, sB, rB, sX, rX, sF, rF, sR, rR, sP, rP, sE, rE, sW, rW, sG, rG, sV, rV, sT, rT, ready, go,
 ):
     comp, tile, lev = lax.axis_index("comp"), lax.axis_index("tile"), lax.axis_index("lev")
     tiles = lax.axis_size("tile")
@@ -78,6 +78,7 @@
     is_wrap = jnp.logical_or(first, last)
     order = half * 2 + jnp.where(last, 1, 0)
     is_teller = jnp.logical_and(comp >= 2, x == 1)
+    is_late_sky = jnp.logical_and(is_sky, half == 1)
     is_early = jnp.logical_and(half == 0, tile < tiles // 2)
     is_hub = jnp.logical_and(first, half == 0)
     x_peers = [half * 4 + lax.rem(x + k, 4) for k in range(1, 4)]
@@ -248,6 +249,9 @@
         def _():
             send(sendB.at[0], relayB.at[1], sW, rV.at[1], tile=0, lev=x)
 
+    here = jnp.logical_and(iota((16, 80), 0) < 10, iota((16, 80), 1) == lev * 10 + iota((16, 80), 0))
+    top_row = jnp.broadcast_to(m_v[0:1, :], (16, 80))
+    scale = jnp.sum(jnp.where(here, top_row, 0.0), axis=1, keepdims=True)
     picked = dot(pick_rows, m_v[...])
     matrix = dot(picked, pick_cols(64, half * 40))
 
@@ -259,12 +263,10 @@
     @pl.when(tile > 0)
     def _():
         drain(haloA.at[0], rA.at[0])
-        drain(haloB.at[0], rB.at[0])
 
     @pl.when(tile < tiles - 1)
     def _():
         drain(haloA.at[1], rA.at[1])
-        drain(haloB.at[1], rB.at[1])
 
     for k, block in enumerate(joined(haloA[1], haloA[0])):
         ext[k, :, 512:640] = block
@@ -277,6 +279,15 @@
     heat = heat_step(ext[0], up, un, ext[2])
     heat = heat_step(heat, up * sky, un * sky, ext[2] * sky)[:, 0:512]
 
+    @pl.when(is_late_sky)
+    def _():
+        part = jnp.sum(heat * scale, axis=0, keepdims=True)
+        for c in range(4):
+            parts[c] = part[:, c * 128 : (c + 1) * 128]
+        landed[x] = parts[x]
+        for k in range(3):
+            send(parts.at[lax.rem(x + k + 1, 4)], landed.at[x], sT.at[k], rT.at[k], lev=x_peers[k])
+
     def level(r):
         edge = jnp.where(
             low40,
@@ -295,13 +306,49 @@
 
         lax.fori_loop(1, 10, more, 0)
 
+    row8 = iota((8, 512), 0)
+    gath[x, 0:8, :] = heat[0:8]
+    gath[x, 8:16, :] = jnp.where(row8 < 2, heat[8:16], 0.0)
+
+    def share():
+        for k in range(3):
+            send(gath.at[x], gath.at[x], sX.at[k], rX.at[k], lev=x_peers[k])
+
+    @pl.when(half == 1)
+    def _():
+        share()
+
+    @pl.when(tile > 0)
+    def _():
+        drain(haloB.at[0], rB.at[0])
+
+    @pl.when(tile < tiles - 1)
+    def _():
+        drain(haloB.at[1], rB.at[1])
+
     level(0)
-    row8 = iota((8, 512), 0)
-    rows_q = pltpu.roll(qout[0, 0:8, :], 2, 0)
-    gath[x, 0:8, :] = heat[0:8]
-    gath[x, 8:16, :] = jnp.where(row8 < 2, heat[8:16], jnp.where(row8 < 5, rows_q, 0.0))
-    for k in range(3):
-        send(gath.at[x], gath.at[x], sX.at[k], rX.at[k], lev=x_peers[k])
+
+    @pl.when(half == 0)
+    def _():
+        rows_q = pltpu.roll(qout[0, 0:8, :], 2, 0)
+        gath[x, 8:16, :] = jnp.where(row8 < 2, heat[8:16], jnp.where(row8 < 5, rows_q, 0.0))
+        share()
+
+    def late_rows(start, stop):
+        def body(k, _):
+            send(piece, pieces.at[x, tile], sP, rP, comp=comp + 2, tile=k, lev=0)
+            return 0
+
+        lax.fori_loop(start, stop, body, 0)
+
+    @pl.when(is_late_sky)
+    def _():
+        for k in range(3):
+            drain(landed.at[k], rT.at[k])
+        piece[...] = landed[0] + landed[1] + landed[2] + landed[3]
+        pl.semaphore_wait(go, 1)
+        late_rows(0, 8)
+
     for k in range(3):
         drain(gath.at[k], rX.at[k])
     product = dot(matrix, jnp.concatenate([gath[k] for k in range(4)], axis=0))
@@ -311,24 +358,9 @@
     def _():
         tracers_inside()
 
-    @pl.when(is_sky)
+    @pl.when(jnp.logical_and(is_sky, half == 0))
     def _():
         pl.semaphore_wait(go, 1)
-
-    @pl.when(jnp.logical_and(is_sky, half == 1))
-    def _():
-        piece[...] = jnp.where(
-            x == 0, top[:, 0:128], jnp.where(x == 1, top[:, 128:256], jnp.where(x == 2, top[:, 256:384], top[:, 384:512]))
-        )
-
-        def body(k, _):
-            send(piece, pieces.at[x, tile], sP, rP, comp=comp + 2, tile=k, lev=0)
-            return 0
-
-        lax.fori_loop(0, tiles, body, 0)
-
-    @pl.when(jnp.logical_and(is_sky, half == 0))
-    def _():
         line = jnp.where(
             x == 0, gath[0, 10:11, :], jnp.where(x == 1, gath[0, 11:12, :], jnp.where(x == 2, gath[0, 12:13, :], top))
         )
@@ -348,6 +380,10 @@
     @pl.when(half == 1)
     def _():
         send(flip_s, flip_r, sF, rF, lev=other)
+
+    @pl.when(is_late_sky)
+    def _():
+        late_rows(8, tiles)
 
     def edge_heat(from_right, from_left, again):
         t, u, d = joined(from_right, from_left)
@@ -518,6 +554,8 @@
     @pl.when(jnp.logical_and(is_sky, half == 1))
     def _():
         drain(pieces.at[0], sP)
+        for k in range(3):
+            drain(parts.at[k], sT.at[k])
 
     @pl.when(is_wrap)
     def _():
@@ -557,9 +595,9 @@
             buf(4, 16, 512), buf(40, 128), buf(40, 128), buf(16, 512), buf(4, 128), buf(1, 128),
             buf(4, tiles, 4, 128), buf(4, tiles, 1, 128),
             buf(4, 4, 16, 128), buf(4, 16, 128), buf(40, 128), buf(8, 128), buf(8, 128), buf(32, 128), buf(16, 128),
-            buf(2, 40, 128), buf(3, 2, 16, 128), buf(2, 16, 128),
+            buf(2, 40, 128), buf(3, 2, 16, 128), buf(2, 16, 128), buf(4, 1, 128), buf(4, 1, 128),
             dma((9,)), dma((2,)), dma((2,)), dma((2,)), dma((2,)), dma((3,)), dma((3,)), dma, dma,
-            dma, dma, dma, dma, dma((4,)), dma((4,)), dma, dma, dma, dma, dma((3,)), dma((2,)), pltpu.SemaphoreType.REGULAR, pltpu.SemaphoreType.REGULAR,
+            dma, dma, dma, dma, dma((4,)), dma((4,)), dma, dma, dma, dma, dma((3,)), dma((2,)), dma((3,)), dma((3,)), pltpu.SemaphoreType.REGULAR, pltpu.SemaphoreType.REGULAR,
         ],
         compiler_params=pltpu.CompilerParams(
             collective_id=0, has_side_effects=True, vmem_limit_bytes=24 * 1024 * 1024

time: 46 us -> 45.6 us (level)
  no operation moved by 1% of the time
where the time goes in v5:
time: 45.6 us; the launch traced here: 45.4 us
  Pallas kernels  43.3 us (95%)
  local copies, waits for them, and re-layouts  1.5 us (3%)
  between operations  0.64 us (1%)
    pallas_call x1, Pallas kernels, body(): pl.pallas_call(kernel, out_shape=(jax.ShapeDtypeStruct((40, 128), F32), j...  43.3 us
    unnamed x2, local copies, waits for them, and re-layouts  1.5 us

profile of v5, /device:TPU:1, one launch (start us, length us, event | category | flops | bytes accessed | tf_op | source)
XLA Modules:
  0.0 45.4 jit_solution(12992821951500603441)
XLA Ops:
  0.6 43.3 %shard_map.95 = (f32[40,128]{1,0:T(8,128)S(1)}, f32[10,40,512]{2,1,0:T(8,128)S(1)}) custom-call(f32[40,128]{1,0:T(8,128)} %bitcast.18, f32[40,128]{1,0:T(8,128)} %bitcast.19, f32[40,128]{1,0:T(8,128)} %bitcast.20, f32[10,40,512]{2,1,0:T(8,128)} %bitcast.16, f32[80,80]{1,0:T(8,128)} %bitcast.17, f32[4,512]{1,0:T(4,128)} %bitcast.21, s32[4,512]{1,0:T(4,128)} %bitcast.22, ...), custom_call_target="tpu_custom_call" | custom-call | tf_op jit(solution)/shard_map/pallas_call | solution.py:586
  43.9 0.6 %copy.14 = f32[1,10,512]{2,0,1:T(1,128)} copy(f32[1,10,512]{2,0,1:T(1,128)S(1)} %bitcast.15) | data formatting | bytes 40960
  44.5 0.9 %copy.15 = f32[1,40,10,512]{3,1,2,0:T(8,128)} copy(f32[1,40,10,512]{3,1,2,0:T(8,128)S(1)} %bitcast.14) | data formatting | bytes 1638400

commit v6 on v5

--- a/solution.py
+++ b/solution.py
@@ -67,7 +67,7 @@
     t40, u40, d40, qin, m_v, w_v, i_v, i_s, sea_v,
     ext, coef, sendA, sendB, haloA, haloB, gath, flip_s, flip_r, own, srow, piece, rows, pieces,
     ring, ring_coef, wrapB, edge_s, edge_rows, mixed_rows, mixed_v, relayB, answer, reply, parts, landed,
-    in_sem, sA, rA, sB, rB, sX, rX, sF, rF, sR, rR, sP, rP, sE, rE, sW, rW, sG, rG, sV, rV, sT, rT, ready, go,
+    in_sem, sA, rA, sB, rB, sX, rX, sF, rF, sR, rR, sP, rP, sE, rE, sW, rW, sG, rG, sV, rV, sT, rT, ready, go, hub_up,
 ):
     comp, tile, lev = lax.axis_index("comp"), lax.axis_index("tile"), lax.axis_index("lev")
     tiles = lax.axis_size("tile")
@@ -111,17 +111,21 @@
     for p in x_peers:
         hello(lev=p)
 
-    @pl.when(half == 0)
+    @pl.when(jnp.logical_and(half == 0, tile > 0))
     def _():
         hello(lev=lev + 4)
 
+    @pl.when(jnp.logical_and(half == 1, first))
+    def _():
+        hello(tile=tiles - 1, lev=x)
+
     @pl.when(is_sky)
     def _():
         hello(comp=comp + 2, lev=half * 4 + 1)
 
     @pl.when(is_hub)
     def _():
-        for g in range(1, 4):
+        for g in (1, 3):
             for k in range(4):
                 hello(**group(g, k))
 
@@ -183,8 +187,8 @@
         haloB[1] = zero40
 
     greeted = (
-        jnp.where(tile > 0, 1, 0) + jnp.where(tile < tiles - 1, 1, 0) + 3 + half
-        + jnp.where(is_teller, tiles + 4 - jnp.where(half == 0, 1, 0), 0) + jnp.where(jnp.logical_and(is_wrap, order > 0), 4, 0)
+        jnp.where(tile > 0, 1, 0) + jnp.where(tile < tiles - 1, 1, 0) + 3 + jnp.where(first, 0, half)
+        + jnp.where(is_teller, tiles + 4 - jnp.where(half == 0, 1, 0), 0) + jnp.where(last, 5 - half, 0)
     )
     pl.semaphore_wait(bar, greeted)
 
@@ -198,7 +202,12 @@
         send(sendA.at[1], haloA.at[1], sA.at[1], rA.at[1], tile=tile - 1)
         send(sendB.at[1], haloB.at[1], sB.at[1], rB.at[1], tile=tile - 1)
 
-    @pl.when(half == 1)
+    @pl.when(jnp.logical_and(half == 0, last))
+    def _():
+        where = {"tile": 0, "lev": 4 + x}
+        pl.semaphore_signal(hub_up, inc=1, device_id=where, device_id_type=MESH)
+
+    @pl.when(jnp.logical_and(half == 1, tile > 0))
     def _():
         pl.semaphore_signal(ready, inc=1, device_id={"lev": lev - 4}, device_id_type=MESH)
 
@@ -232,7 +241,7 @@
             for p in x_peers:
                 send(mine, mine, sE.at[0], rE.at[0], lev=p)
 
-        @pl.when(order > 0)
+        @pl.when(last)
         def _():
             for k in range(4):
                 send(mine, mine, sE.at[0], rE.at[order], **group(0, k))
@@ -240,10 +249,6 @@
         @pl.when(order == 1)
         def _():
             send(sendB.at[0], wrapB, sW, rW, tile=0)
-
-        @pl.when(order == 2)
-        def _():
-            send(sendB.at[1], relayB.at[0], sW, rV.at[0], tile=0, lev=x)
 
         @pl.when(order == 3)
         def _():
@@ -317,6 +322,15 @@
     @pl.when(half == 1)
     def _():
         share()
+
+    @pl.when(jnp.logical_and(half == 1, first))
+    def _():
+        pl.semaphore_wait(hub_up, 1)
+        pl.semaphore_signal(ready, inc=1, device_id={"lev": lev - 4}, device_id_type=MESH)
+        mine = ring.at[2, x]
+        for k in range(4):
+            send(mine, mine, sE.at[0], rE.at[2], **group(0, k))
+        send(sendB.at[1], relayB.at[0], sW, rV.at[0], tile=0, lev=x)
 
     @pl.when(tile > 0)
     def _():
@@ -597,7 +611,7 @@
             buf(4, 4, 16, 128), buf(4, 16, 128), buf(40, 128), buf(8, 128), buf(8, 128), buf(32, 128), buf(16, 128),
             buf(2, 40, 128), buf(3, 2, 16, 128), buf(2, 16, 128), buf(4, 1, 128), buf(4, 1, 128),
             dma((9,)), dma((2,)), dma((2,)), dma((2,)), dma((2,)), dma((3,)), dma((3,)), dma, dma,
-            dma, dma, dma, dma, dma((4,)), dma((4,)), dma, dma, dma, dma, dma((3,)), dma((2,)), dma((3,)), dma((3,)), pltpu.SemaphoreType.REGULAR, pltpu.SemaphoreType.REGULAR,
+            dma, dma, dma, dma, dma((4,)), dma((4,)), dma, dma, dma, dma, dma((3,)), dma((2,)), dma((3,)), dma((3,)), pltpu.SemaphoreType.REGULAR, pltpu.SemaphoreType.REGULAR, pltpu.SemaphoreType.REGULAR,
         ],
         compiler_params=pltpu.CompilerParams(
             collective_id=0, has_side_effects=True, vmem_limit_bytes=24 * 1024 * 1024

time: 45.6 us -> 45 us (0.987)
  the two profiles are of different devices: /device:TPU:1 before, /device:TPU:2 now
where the time goes in v6:
time: 45 us; the launch traced here: 44.8 us
  Pallas kernels  42.7 us (95%)
  local copies, waits for them, and re-layouts  1.5 us (3%)
  between operations  0.64 us (1%)
    pallas_call x1, Pallas kernels, body(): pl.pallas_call(kernel, out_shape=(jax.ShapeDtypeStruct((40, 128), F32), j...  42.7 us
    unnamed x2, local copies, waits for them, and re-layouts  1.5 us

profile of v6, /device:TPU:2, one launch (start us, length us, event | category | flops | bytes accessed | tf_op | source)
XLA Modules:
  0.0 44.8 jit_solution(12413331150997853220)
XLA Ops:
  0.6 42.7 %shard_map.95 = (f32[40,128]{1,0:T(8,128)S(1)}, f32[10,40,512]{2,1,0:T(8,128)S(1)}) custom-call(f32[40,128]{1,0:T(8,128)} %bitcast.18, f32[40,128]{1,0:T(8,128)} %bitcast.19, f32[40,128]{1,0:T(8,128)} %bitcast.20, f32[10,40,512]{2,1,0:T(8,128)} %bitcast.16, f32[80,80]{1,0:T(8,128)} %bitcast.17, f32[4,512]{1,0:T(4,128)} %bitcast.21, s32[4,512]{1,0:T(4,128)} %bitcast.22, ...), custom_call_target="tpu_custom_call" | custom-call | tf_op jit(solution)/shard_map/pallas_call | solution.py:600
  43.3 0.6 %copy.14 = f32[1,10,512]{2,0,1:T(1,128)} copy(f32[1,10,512]{2,0,1:T(1,128)S(1)} %bitcast.15) | data formatting | bytes 40960
  43.9 0.9 %copy.15 = f32[1,40,10,512]{3,1,2,0:T(8,128)} copy(f32[1,40,10,512]{3,1,2,0:T(8,128)S(1)} %bitcast.14) | data formatting | bytes 1638400

commit v7 on v6

--- a/solution.py
+++ b/solution.py
@@ -404,61 +404,7 @@
         up, un = courant(u)
         return heat_step(heat_step(t, up, un, d), up * again, un * again, d * again)
 
-    @pl.when(is_hub)
-    def _():
-        drain(ring.at[0, pl.ds(0, 3)], rE.at[0])
-        for g in range(1, 4):
-            drain(ring.at[g], rE.at[g])
-        stepped = [edge_heat(ring[2 * (k // 4), k % 4], ring[2 * (k // 4) + 1, k % 4], sky) for k in range(8)]
-        mixed = dot(mixed_rows[...], jnp.concatenate(stepped, axis=0))
-        mixed_v[...] = mixed[0:16]
-
-        @pl.when(jnp.logical_and(is_sky, lev == 0))
-        def _():
-            q, u, _ = joined(ring[0, 0], ring[1, 0])
-            up, un = courant(jnp.broadcast_to(u[0:1], (8, 128)))
-            edge_s[...] = tracer_step(tracer_step(q[8:16], up, un), up, un)
-            edge_s[0:1, :] = mixed_v[0:1, :]
-
-            def body(k, _):
-                send(edge_s, edge_rows, sG, rG, comp=comp + 2, tile=k, lev=0)
-                return 0
-
-            lax.fori_loop(0, tiles, body, 0)
-
-        answer[0, 0] = mixed[0:16]
-        answer[1, 0] = mixed[16:32]
-        answer[2, 0] = mixed[16:32]
-        answer[0, 1] = ring[0, x]
-        answer[1, 1] = ring[3, x]
-        answer[2, 1] = ring[2, x]
-        for g in range(1, 4):
-            send(answer.at[g - 1], reply, sE.at[g], rE.at[0], **group(g, x))
-        for k in range(2):
-            drain(relayB.at[k], rV.at[k])
-        for g, edge in ((1, sendB.at[1]), (2, relayB.at[1]), (3, relayB.at[0])):
-            send(edge, wrapB, sV.at[g - 1], rW, **group(g, x))
-
-    @pl.when(jnp.logical_not(is_early))
-    def _():
-        tracers_inside()
-
-    @pl.when(half == 0)
-    def _():
-        pl.semaphore_wait(ready, 1)
-        send(flip_s, flip_r, sF, rF, lev=other)
-
-    for c in loads[5:]:
-        c.wait()
-
-    @pl.when(jnp.logical_and(is_wrap, order > 0))
-    def _():
-        drain(reply, rE.at[0])
-        mixed_v[...] = reply[0]
-        ring[half * 2 + jnp.where(last, 0, 1), x] = reply[1]
-
-    @pl.when(is_wrap)
-    def _():
+    def wrapped_tracers():
         drain(wrapB, rW)
         up, un = courant(joined(ring[half * 2, x], ring[half * 2 + 1, x])[1])
         ring_coef[0] = up
@@ -482,6 +428,65 @@
                     return 0
 
                 lax.fori_loop(0, 10, fix, 0)
+
+    @pl.when(is_hub)
+    def _():
+        drain(ring.at[0, pl.ds(0, 3)], rE.at[0])
+        drain(ring.at[1], rE.at[1])
+        wrapped_tracers()
+        for g in (2, 3):
+            drain(ring.at[g], rE.at[g])
+        stepped = [edge_heat(ring[2 * (k // 4), k % 4], ring[2 * (k // 4) + 1, k % 4], sky) for k in range(8)]
+        mixed = dot(mixed_rows[...], jnp.concatenate(stepped, axis=0))
+        mixed_v[...] = mixed[0:16]
+
+        @pl.when(jnp.logical_and(is_sky, lev == 0))
+        def _():
+            q, u, _ = joined(ring[0, 0], ring[1, 0])
+            up, un = courant(jnp.broadcast_to(u[0:1], (8, 128)))
+            edge_s[...] = tracer_step(tracer_step(q[8:16], up, un), up, un)
+            edge_s[0:1, :] = mixed_v[0:1, :]
+
+            def body(k, _):
+                send(edge_s, edge_rows, sG, rG, comp=comp + 2, tile=k, lev=0)
+                return 0
+
+            lax.fori_loop(0, tiles, body, 0)
+
+        answer[0, 0] = mixed[0:16]
+        answer[1, 0] = mixed[16:32]
+        answer[2, 0] = mixed[16:32]
+        answer[0, 1] = ring[0, x]
+        answer[1, 1] = ring[3, x]
+        answer[2, 1] = ring[2, x]
+        for g in range(1, 4):
+            send(answer.at[g - 1], reply, sE.at[g], rE.at[0], **group(g, x))
+        for k in range(2):
+            drain(relayB.at[k], rV.at[k])
+        for g, edge in ((1, sendB.at[1]), (2, relayB.at[1]), (3, relayB.at[0])):
+            send(edge, wrapB, sV.at[g - 1], rW, **group(g, x))
+
+    @pl.when(jnp.logical_not(is_early))
+    def _():
+        tracers_inside()
+
+    @pl.when(half == 0)
+    def _():
+        pl.semaphore_wait(ready, 1)
+        send(flip_s, flip_r, sF, rF, lev=other)
+
+    for c in loads[5:]:
+        c.wait()
+
+    @pl.when(jnp.logical_and(is_wrap, order > 0))
+    def _():
+        drain(reply, rE.at[0])
+        mixed_v[...] = reply[0]
+        ring[half * 2 + jnp.where(last, 0, 1), x] = reply[1]
+
+    @pl.when(jnp.logical_and(is_wrap, order > 0))
+    def _():
+        wrapped_tracers()
 
     block = lax.shift_right_logical(i_s[0, 256], 9)
     before, after = lax.rem(block + tiles - 1, tiles), lax.rem(block + 1, tiles)

time: 45 us -> 44.9 us (level)
  the two profiles are of different devices: /device:TPU:2 before, /device:TPU:17 now
where the time goes in v7:
time: 44.9 us; the launch traced here: 44.8 us
  Pallas kernels  42.6 us (95%)
  local copies, waits for them, and re-layouts  1.5 us (3%)
  between operations  0.64 us (1%)
    pallas_call x1, Pallas kernels, body(): pl.pallas_call(kernel, out_shape=(jax.ShapeDtypeStruct((40, 128), F32), j...  42.6 us
    unnamed x2, local copies, waits for them, and re-layouts  1.5 us

profile of v7, /device:TPU:17, one launch (start us, length us, event | category | flops | bytes accessed | tf_op | source)
XLA Modules:
  0.0 44.8 jit_solution(5135490544063235814)
XLA Ops:
  0.6 42.6 %shard_map.95 = (f32[40,128]{1,0:T(8,128)S(1)}, f32[10,40,512]{2,1,0:T(8,128)S(1)}) custom-call(f32[40,128]{1,0:T(8,128)} %bitcast.18, f32[40,128]{1,0:T(8,128)} %bitcast.19, f32[40,128]{1,0:T(8,128)} %bitcast.20, f32[10,40,512]{2,1,0:T(8,128)} %bitcast.16, f32[80,80]{1,0:T(8,128)} %bitcast.17, f32[4,512]{1,0:T(4,128)} %bitcast.21, s32[4,512]{1,0:T(4,128)} %bitcast.22, ...), custom_call_target="tpu_custom_call" | custom-call | tf_op jit(solution)/shard_map/pallas_call | solution.py:605
  43.3 0.6 %copy.14 = f32[1,10,512]{2,0,1:T(1,128)} copy(f32[1,10,512]{2,0,1:T(1,128)S(1)} %bitcast.15) | data formatting | bytes 40960
  43.9 0.9 %copy.15 = f32[1,40,10,512]{3,1,2,0:T(8,128)} copy(f32[1,40,10,512]{3,1,2,0:T(8,128)S(1)} %bitcast.14) | data formatting | bytes 1638400
